TPU v7x, 256 devices: a whole 4x4x8 slice. The times are simulated.
256 devices in a mesh: row: 2 (over core), cube: 128 (over y, x, z).
Axes of the slice: x: 4, y: 4, z: 8, core: 2. Of those that a mesh axis runs over, the one named last changes fastest.
Arguments:
- child_fronts: float32 [128, 96, 2, 3072], P('cube', None, 'row'), as said below
- root_front: float32 [128, 80, 2, 5120], P('cube', None, 'row'), as said below
- child_map: int32 [2, 23], replicated, may hold values from 0 to 39, as said below
Outputs:
- child_factor: float32 [128, 4, 2, 3072], P('cube', None, 'row')
- root_factor: float32 [128, 2, 2, 5120], P('cube', None, 'row')
- root_rest: float32 [128, 78, 2, 4992], P('cube', None, 'row')
Inputs may be any that keep to these rules, and one draw needn't show every extreme that they name: `child_fronts`: each F_c is symmetric positive definite. `root_front`: A is symmetric positive definite. `child_map`: each row names 23 different blocks; both rows name block 0 and block 39.
All inputs are finite; a program needn't handle non-finite values.
Results may differ from a plain program's by a relative error of at most 0.0001.
Values sent between devices are 32-bit elements; how exact they have to be, the bound alone decides.
A program may use at most 128 MiB of HBM per device.

v0:
```python
import jax
import jax.numpy as jnp
from jax import lax
from jax.sharding import PartitionSpec as P

PANEL = 128
BLOCK = 256
CHILD_PANELS = 2
ROOT_PANELS = 2
CHILD_PIVOTS = 256
ROOT_PIVOTS = 256
UPDATE_BLOCKS = 23
ROOT_BLOCKS = 40


PRECISE = lax.Precision.HIGHEST


def swapped(block, axis, apart):
    count = lax.axis_size(axis)
    route = []
    for low in range(count):
        high = low | 1 << apart
        if high != low and high < count:
            route += [(low, high), (high, low)]
    return lax.ppermute(block, axis, route)


def collect(pivot_rows, members):
    position = lax.axis_index("cube")
    gathered = lax.all_gather(pivot_rows, "cube", axis=0, tiled=True)
    if members == lax.axis_size("cube"):
        return gathered
    first_member = position // members * members
    return lax.dynamic_slice_in_dim(gathered, first_member, members, 0)


def eliminate(front_rows, members, panels):
    within = lax.axis_index("cube") % members
    halves = lax.axis_size("row")
    slot_count, columns = front_rows.shape
    stride = PANEL // members
    trailing = front_rows
    factor_parts = []
    for panel_index in range(panels):
        gathered = collect(trailing[:stride][None], members)
        pivot_block = jnp.transpose(gathered, (1, 0, 2)).reshape(PANEL, columns)
        first_column = panel_index * PANEL // halves
        diagonal_half = pivot_block[:, first_column : first_column + PANEL // halves]
        own_columns = pivot_block.reshape(PANEL, slot_count, members // halves)
        own_columns = lax.dynamic_index_in_dim(own_columns, within // halves, 2, keepdims=False)
        diagonal_parts, own_parts = (
            lax.all_gather(diagonal_half[None], "row", axis=0, tiled=True),
            lax.all_gather(own_columns[None], "row", axis=0, tiled=True),
        )
        diagonal = jnp.transpose(diagonal_parts, (1, 2, 0)).reshape(PANEL, PANEL)
        own_full = lax.dynamic_index_in_dim(own_parts, within % halves, 0, keepdims=False)
        lower_factor = jnp.linalg.cholesky(diagonal)
        factor_block = lax.linalg.triangular_solve(
            lower_factor, pivot_block, left_side=True, lower=True
        )
        factor_own = lax.linalg.triangular_solve(lower_factor, own_full, left_side=True, lower=True)
        mine_factor = lax.dynamic_index_in_dim(
            factor_block.reshape(stride, members, columns), within, 1, keepdims=False
        )
        factor_parts.append(mine_factor)
        finished = (panel_index + 1) * stride
        remaining = trailing[stride:]
        coupling = factor_own[:, finished:]
        trailing = remaining - jnp.einsum("pr,pc->rc", coupling, factor_block, precision=PRECISE)
    return (trailing, jnp.concatenate(factor_parts, 0))


def place_blocks(pieces, mapping):
    targets = lax.broadcasted_iota(jnp.int32, (ROOT_BLOCKS, mapping.shape[0]), 0)
    selector = (targets == mapping[None, :]).astype(jnp.float32)
    spread = jnp.einsum("mu,usvb->msvb", selector, pieces, precision=PRECISE)
    spread = jnp.einsum("nv,msvb->msnb", selector, spread, precision=PRECISE)
    return spread.reshape(ROOT_BLOCKS * pieces.shape[1], ROOT_BLOCKS * pieces.shape[3])


def shards(child_fronts, root_front, child_map):
    position = lax.axis_index("cube")
    members = lax.axis_size("cube") // 2
    halves = lax.axis_size("row")
    child_rest, child_factor = eliminate(child_fronts[0, :, 0, :], members, CHILD_PANELS)
    pivot_columns = CHILD_PIVOTS // halves
    per_block = BLOCK // (2 * members)
    block_width = BLOCK // halves
    update = child_rest[:, pivot_columns:].reshape(
        UPDATE_BLOCKS, per_block, 2, UPDATE_BLOCKS, block_width
    )
    own_child = position // members
    staying = lax.dynamic_index_in_dim(update, own_child, 2, keepdims=False)
    leaving = lax.dynamic_index_in_dim(update, 1 - own_child, 2, keepdims=False)
    arrived = swapped(leaving, "cube", members.bit_length() - 1)
    own_map = lax.dynamic_index_in_dim(child_map, own_child, 0, keepdims=False)
    other_map = lax.dynamic_index_in_dim(child_map, 1 - own_child, 0, keepdims=False)
    assembled = (
        root_front[0, :, 0, :] + place_blocks(staying, own_map) + place_blocks(arrived, other_map)
    )
    root_trailing, root_factor = eliminate(assembled, 2 * members, ROOT_PANELS)
    root_rest = root_trailing[:, ROOT_PIVOTS // halves :]
    return (
        child_factor[None, :, None, :],
        root_factor[None, :, None, :],
        root_rest[None, :, None, :],
    )


def solution(mesh):
    placed = (P("cube", None, "row", None), P("cube", None, "row", None), P())
    return jax.shard_map(
        shards,
        mesh=mesh,
        in_specs=placed,
        out_specs=(
            P("cube", None, "row", None),
            P("cube", None, "row", None),
            P("cube", None, "row", None),
        ),
        check_vma=False,
    )
```

profile of v0, /device:TPU:2, one launch (start us, length us, event | category | flops | bytes accessed | tf_op | source)
XLA Modules:
  0.0 667.4 jit_solution(11821123723109811660)
XLA Ops:
  8.7 2.3 slice.72
  11.0 119.1 %all-gather.20.cloned.1.call-done = f32[128,2,1,3072]{3,1,2,0:T(2,128)} async-done(((f32[1,2,1,3072]{3,1,2,0:T(2,128)}), f32[128,2,1,3072]{3,1,2,0:T(2,128)}) %all-gather.20.cloned.1.call-update) | async-done | bytes 3145744 | tf_op jit(solution)/shard_map/all_gather | solution.py:31
  132.2 1.9 all-gather.1
  134.3 11.7 %cholesky.74 = f32[128,128]{1,0:T(8,128)S(1)} custom-call(f32[128,128]{1,0:T(8,128)S(1)} %add_multiply_fusion.3), custom_call_target="Cholesky" | custom-call | tf_op jit(solution)/shard_map/jit(cholesky)/cholesky | solution.py:58
  147.4 9.8 %custom-call.18 = f32[1,128,128]{1,2,0:T(8,128)S(1)} custom-call(f32[1,128,128]{2,1,0:T(8,128)S(1)} %fusion.10), custom_call_target="InvertDiagBlocksLowerTriangular" | custom-call | tf_op jit(solution)/shard_map/triangular_solve/custom-call.0 | solution.py:59
  158.7 3.6 copy.76
  162.3 3.4 reshape_reshape.6
  165.7 1.9 all-gather.2
  167.9 2.5 convolution_subtract_fusion.1
  172.5 111.1 %all-gather.22.cloned.1.call-done = f32[128,2,3072]{2,1,0:T(2,128)} async-done(((f32[1,2,3072]{2,1,0:T(2,128)}), f32[128,2,3072]{2,1,0:T(2,128)}) %all-gather.22.cloned.1.call-update) | async-done | bytes 3145744 | tf_op jit(solution)/shard_map/all_gather | solution.py:31
  285.7 1.9 all-gather.4
  287.8 11.7 %cholesky.85 = f32[128,128]{1,0:T(8,128)S(1)} custom-call(f32[128,128]{1,0:T(8,128)S(1)} %add_multiply_fusion.2), custom_call_target="Cholesky" | custom-call | tf_op jit(solution)/shard_map/jit(cholesky)/cholesky | solution.py:58
  300.8 9.8 %custom-call.20 = f32[1,128,128]{1,2,0:T(8,128)S(1)} custom-call(f32[1,128,128]{2,1,0:T(8,128)S(1)} %fusion.11), custom_call_target="InvertDiagBlocksLowerTriangular" | custom-call | tf_op jit(solution)/shard_map/triangular_solve/custom-call.0 | solution.py:59
  312.1 3.6 copy.80
  315.7 3.4 reshape_reshape.7
  319.2 2.0 all-gather.5
  323.2 2.1 collective-permute-start
  327.0 12.2 %collective-permute-done = f32[23,2,23,128]{3,1,2,0:T(2,128)S(1)} collective-permute-done((f32[23,2,23,128]{3,1,2,0:T(2,128)S(1)}, f32[23,2,23,128]{3,1,2,0:T(2,128)S(1)}, u32[]{:S(2)}, u32[]{:S(2)}) %collective-permute-start) | collective-permute-done | bytes 541728 | tf_op jit(solution)/shard_map/ppermute | solution.py:26
  344.0 112.2 %all-gather.24.cloned.1.call-done = f32[128,1,5120]{2,1,0:T(1,128)} async-done(((f32[1,1,5120]{2,1,0:T(1,128)}), f32[128,1,5120]{2,1,0:T(1,128)}) %all-gather.24.cloned.1.call-update) | async-done | bytes 2621456 | tf_op jit(solution)/shard_map/all_gather | solution.py:31
  456.2 6.6 copy.88
  463.7 1.9 all-gather.8
  466.1 10.5 %all-gather.7 = f32[256,64]{1,0:T(8,128)S(1)} all-gather(f32[128,64]{1,0:T(8,128)S(1)} %slice.102), channel_id=9, replica_groups=mesh['row'=2,'cube'=128] {'row'}, dimensions={0}, use_global_device_ids=true | all-gather | bytes 98304 | tf_op jit(solution)/shard_map/all_gather | solution.py:53
  476.8 11.7 %cholesky.96 = f32[128,128]{1,0:T(8,128)S(1)} custom-call(f32[128,128]{1,0:T(8,128)S(1)} %add_multiply_fusion.1), custom_call_target="Cholesky" | custom-call | tf_op jit(solution)/shard_map/jit(cholesky)/cholesky | solution.py:58
  489.8 9.8 %custom-call.22 = f32[1,128,128]{1,2,0:T(8,128)S(1)} custom-call(f32[1,128,128]{2,1,0:T(8,128)S(1)} %fusion.12), custom_call_target="InvertDiagBlocksLowerTriangular" | custom-call | tf_op jit(solution)/shard_map/triangular_solve/custom-call.3 | solution.py:59
  499.9 2.7 fusion.20
  510.1 107.0 %all-gather.26.cloned.1.call-done = f32[128,1,5120]{2,1,0:T(1,128)} async-done(((f32[1,1,5120]{2,1,0:T(1,128)}), f32[128,1,5120]{2,1,0:T(1,128)}) %all-gather.26.cloned.1.call-update) | async-done | bytes 2621456 | tf_op jit(solution)/shard_map/all_gather | solution.py:31
  617.1 6.6 copy.91
  627.1 2.1 all-gather.10
  629.4 11.7 %cholesky.107 = f32[128,128]{1,0:T(8,128)S(1)} custom-call(f32[128,128]{1,0:T(8,128)S(1)} %add_multiply_fusion), custom_call_target="Cholesky" | custom-call | tf_op jit(solution)/shard_map/jit(cholesky)/cholesky | solution.py:58
  642.5 9.8 %custom-call.24 = f32[1,128,128]{1,2,0:T(8,128)S(1)} custom-call(f32[1,128,128]{2,1,0:T(8,128)S(1)} %fusion.13), custom_call_target="InvertDiagBlocksLowerTriangular" | custom-call | tf_op jit(solution)/shard_map/triangular_solve/custom-call.3 | solution.py:59
  652.5 2.7 fusion.16
  657.1 2.7 copy.93
  (109 shorter events, 40.6 us)
Async XLA Ops:
  7.2 123.0 %all-gather.20.cloned.1.call-start = ((), (), s32[]{:S(2)}) async-start(), calls=%async_computation | async-start | bytes 3170304 | tf_op jit(solution)/shard_map/all_gather | solution.py:31
  8.6 274.9 %all-gather.22.cloned.1.call-start = ((), (), s32[]{:S(2)}) async-start(), calls=%async_computation.1 | async-start | bytes 3170304 | tf_op jit(solution)/shard_map/all_gather | solution.py:31
  158.7 9.2 %copy-start.6 = (f32[128,3072]{1,0:T(8,128)}, f32[128,3072]{1,0:T(8,128)S(1)}, u32[]{:S(2)}) copy-start(f32[128,3072]{1,0:T(8,128)S(1)} %fusion.28) | copy-start | bytes 4718596
  167.9 3.5 copy-start.10
  171.0 285.2 %all-gather.24.cloned.1.call-start = ((), (), s32[]{:S(2)}) async-start(), calls=%async_computation.2 | async-start | bytes 2641920 | tf_op jit(solution)/shard_map/all_gather | solution.py:31
  312.1 9.3 %copy-start.7 = (f32[128,3072]{1,0:T(8,128)}, f32[128,3072]{1,0:T(8,128)S(1)}, u32[]{:S(2)}) copy-start(f32[128,3072]{1,0:T(8,128)S(1)} %fusion.24) | copy-start | bytes 4718596
  319.1 3.5 copy-start.8
  323.2 16.0 %collective-permute-start = (f32[23,2,23,128]{3,1,2,0:T(2,128)S(1)}, f32[23,2,23,128]{3,1,2,0:T(2,128)S(1)}, u32[]{:S(2)}, u32[]{:S(2)}) collective-permute-start(f32[23,2,23,128]{3,1,2,0:T(2,128)S(1)} %copy.83), channel_id=1, source_target_pairs={{0,64},{64,0},{1,65},{65,1},{2,66},{66,2},{3,67},{67,3},{4,68},{68... | collective-permute-start | bytes 1625096 | tf_op jit(solution)/shard_map/ppermute | solution.py:26
  339.8 1.4 copy-start.9
  342.0 1.2 copy-start.3
  343.9 273.2 %all-gather.26.cloned.1.call-start = ((), (), s32[]{:S(2)}) async-start(), calls=%async_computation.3 | async-start | bytes 2641920 | tf_op jit(solution)/shard_map/all_gather | solution.py:31
  456.2 9.4 %copy-start = (f32[128,1,5120]{2,1,0:T(1,128)S(1)}, f32[128,1,5120]{2,1,0:T(1,128)}, u32[]{:S(2)}) copy-start(f32[128,1,5120]{2,1,0:T(1,128)} %all-gather.24.cloned.1.call-done) | copy-start | bytes 7864324
  499.9 2.7 copy-start.4
  502.6 1.8 copy-start.2
  617.1 9.5 %copy-start.1 = (f32[128,1,5120]{2,1,0:T(1,128)S(1)}, f32[128,1,5120]{2,1,0:T(1,128)}, u32[]{:S(2)}) copy-start(f32[128,1,5120]{2,1,0:T(1,128)} %all-gather.26.cloned.1.call-done) | copy-start | bytes 7864324
  655.2 1.6 copy-start.5
Sparse Core Ops, SparseCore 0:
  12.2 117.8 all-gather.19
  171.1 112.3 all-gather.21
  344.0 112.1 all-gather.23
  505.2 111.8 all-gather.25
where the time goes:
time: 678 us; the launch traced here: 667 us
  waiting for transfers between devices  462 us (68%)
  other arithmetic  92.6 us (14%)
  local copies, waits for them, and re-layouts  52.5 us (8%)
  blocking collectives  24 us (4%)
  matrix products  19.3 us (3%)
  between operations  14.9 us (2%)
    all_gather x4, waiting for transfers between devices, collect(): gathered = lax.all_gather(pivot_rows, 'cube', axis=0, tiled=True)  449 us
    another operation x12, other arithmetic, eliminate(): lower_factor = jnp.linalg.cholesky(diagonal)  49.6 us
    another operation x8, other arithmetic, eliminate(): lax.linalg.triangular_solve(lower_factor, pivot_block, left_side=True, lo...  41.9 us
    all_gather x4, blocking collectives, eliminate(): lax.all_gather(diagonal_half[None], 'row', axis=0, tiled=True)  16.4 us
  transfers between devices with their start and end apart: 5, of which 5 were waited for; matrix products, arithmetic and copies ran while one was open for 2% of the time, Pallas kernels for 0%

commit v1 on v0

v1 whole, which is shorter than its diff:
```python
import functools

import jax
import jax.numpy as jnp
from jax import lax
from jax.experimental import pallas as pl
from jax.experimental.pallas import tpu as pltpu
from jax.sharding import PartitionSpec as P

MESH = pl.DeviceIdType.MESH
LANES = 128
NX = 4
NZ = 8
PIVOTS = 256
UPDATE_BLOCKS = 23
ROOT_BLOCKS = 40
SUB = 64
GROUP = 8
PRECISE = lax.Precision.HIGHEST
VMEM_BYTES = 56 * 2**20
Z_ORDER = (0, 1, 7, 2, 6, 3, 5, 4)
RING = (1, 3, 2)


def dot(a, b, dims=(((1,), (0,)), ((), ()))):
    return lax.dot_general(a, b, dims, precision=PRECISE, preferred_element_type=jnp.float32)


def gather_kernel(slots, ny, cut, x_ref, out_ref, own_sem, z_send, z_recv, p_send, p_recv):
    me = lax.axis_index("cube")
    core = lax.axis_index("row")
    z = me % NZ
    x = me // NZ % NX
    y = me // (NZ * NX)
    ly = y % ny
    base = y - ly
    ring_y = RING if ny == 4 else (1,)

    def chip(py, px, pz):
        return (core, (base + py) * (NX * NZ) + px * NZ + pz)

    def over_x(d):
        return chip(ly, (x + d) % NX, z)

    def over_y(d):
        return chip((ly + d) % ny, x, z)

    def over_z(d):
        return chip(ly, x, (z + d) % NZ)

    barrier = pltpu.get_barrier_semaphore()
    peers = [over_z(d) for d in range(1, NZ)] + [over_x(d) for d in RING] + [over_y(d) for d in ring_y]
    for peer in peers:
        pl.semaphore_signal(barrier, inc=1, device_id=peer, device_id_type=MESH)
    pl.semaphore_wait(barrier, len(peers))

    first = pl.ds(0, cut)
    second = pl.ds(cut, slots - cut)
    started = []

    def send(src, dst, ssem, rsem, peer):
        copy = pltpu.make_async_remote_copy(
            src_ref=src, dst_ref=dst, send_sem=ssem, recv_sem=rsem, device_id=peer, device_id_type=MESH
        )
        copy.start()
        started.append(copy)
        return copy

    mine = pltpu.make_async_copy(x_ref, out_ref.at[:, ly, x, z], own_sem)
    mine.start()
    z_copies = {}
    for d in Z_ORDER[1:]:
        z_copies[d] = send(x_ref, out_ref.at[:, ly, x, z], z_send.at[d], z_recv.at[d], over_z(d))
    mine.wait()
    second_hop = []
    third_hop = []

    def third(t):
        zs = (z + NZ - Z_ORDER[t]) % NZ
        for copy in second_hop[t]:
            copy.wait_recv()
        for k, d in enumerate(ring_y):
            part = out_ref.at[first, ly, :, zs]
            third_hop.append(send(part, part, p_send.at[2, t, k], p_recv.at[2, t, k], over_y(d)))
        for k, d in enumerate(RING):
            part = out_ref.at[second, pl.ds(0, ny), x, zs]
            third_hop.append(send(part, part, p_send.at[3, t, k], p_recv.at[3, t, k], over_x(d)))

    for t, dz in enumerate(Z_ORDER):
        zs = (z + NZ - dz) % NZ
        if dz:
            z_copies[dz].wait_recv()
        hop = []
        for k, d in enumerate(RING):
            part = out_ref.at[first, ly, x, zs]
            hop.append(send(part, part, p_send.at[0, t, k], p_recv.at[0, t, k], over_x(d)))
        for k, d in enumerate(ring_y):
            part = out_ref.at[second, ly, x, zs]
            hop.append(send(part, part, p_send.at[1, t, k], p_recv.at[1, t, k], over_y(d)))
        second_hop.append(hop)
        if t >= 1:
            third(t - 1)
    third(NZ - 1)
    for copy in third_hop:
        copy.wait_recv()
    for copy in started:
        copy.wait_send()


def gather(rows, ny, cut, collective_id):
    slots, groups, lanes = rows.shape
    return pl.pallas_call(
        functools.partial(gather_kernel, slots, ny, cut),
        out_shape=jax.ShapeDtypeStruct((slots, ny, NX, NZ, groups, lanes), jnp.float32),
        in_specs=[pl.BlockSpec(memory_space=pl.ANY)],
        out_specs=pl.BlockSpec(memory_space=pl.ANY),
        scratch_shapes=[
            pltpu.SemaphoreType.DMA,
            pltpu.SemaphoreType.DMA((NZ,)),
            pltpu.SemaphoreType.DMA((NZ,)),
            pltpu.SemaphoreType.DMA((4, NZ, 3)),
            pltpu.SemaphoreType.DMA((4, NZ, 3)),
        ],
        compiler_params=pltpu.CompilerParams(
            collective_id=collective_id, has_side_effects=True, vmem_limit_bytes=VMEM_BYTES
        ),
        name="gather_pivot_rows",
    )(rows)


def interleave(parity):
    k = lax.broadcasted_iota(jnp.int32, (LANES, PIVOTS), 0)
    c = lax.broadcasted_iota(jnp.int32, (LANES, PIVOTS), 1)
    return (c == 2 * k + parity).astype(jnp.float32)


def sub_factor(block):
    rows = [block[i * GROUP : (i + 1) * GROUP] for i in range(SUB // GROUP)]
    sub = lax.broadcasted_iota(jnp.int32, (GROUP, LANES), 0)
    for g in range(SUB // GROUP):
        live = range(g, SUB // GROUP)
        cols = [
            {i: jnp.broadcast_to(rows[i][:, g * GROUP + k : g * GROUP + k + 1], (GROUP, LANES)) for i in live}
            for k in range(GROUP)
        ]
        scale = jnp.zeros((GROUP, LANES), jnp.float32)
        for j in range(GROUP):
            pivot = jnp.broadcast_to(cols[j][g][j : j + 1], (GROUP, LANES))
            inverse = 1.0 / pivot
            scale = jnp.where(sub == j, pivot, scale)
            line = jnp.broadcast_to(rows[g][j : j + 1], (GROUP, LANES))
            heads = {k: jnp.broadcast_to(cols[k][g][j : j + 1], (GROUP, LANES)) for k in range(j + 1, GROUP)}
            for i in live:
                factor = cols[j][i] * inverse
                if i == g:
                    factor = jnp.where(sub > j, factor, 0.0)
                for k in range(j + 1, GROUP):
                    cols[k][i] = cols[k][i] - factor * heads[k]
                rows[i] = rows[i] - factor * line
        root = lax.rsqrt(scale)
        root = root * (1.5 - 0.5 * scale * root * root)
        rows[g] = rows[g] * root
    return jnp.concatenate(rows, 0)[:, SUB:]


def cholesky_kernel(even_ref, odd_ref, inv_ref, d_ref):
    d_ref[...] = dot(even_ref[...], interleave(0)) + dot(odd_ref[...], interleave(1))
    r = lax.broadcasted_iota(jnp.int32, (PIVOTS, PIVOTS), 0)
    c = lax.broadcasted_iota(jnp.int32, (PIVOTS, PIVOTS), 1)
    inv_ref[...] = (r == c).astype(jnp.float32)
    rs = lax.broadcasted_iota(jnp.int32, (SUB, SUB), 0)
    cs = lax.broadcasted_iota(jnp.int32, (SUB, SUB), 1)
    eye = (rs == cs).astype(jnp.float32)
    for o in range(PIVOTS // SUB):
        lo, hi = o * SUB, (o + 1) * SUB
        tile = d_ref[lo:hi, lo:hi]
        small = sub_factor(jnp.concatenate([tile, eye], 1))
        done = dot(small, inv_ref[lo:hi, :])
        inv_ref[lo:hi, :] = done
        if hi < PIVOTS:
            lead = dot(small, d_ref[lo:hi, :])
            tail = lead[:, hi:]
            d_ref[hi:, :] = d_ref[hi:, :] - dot(tail, lead, (((0,), (0,)), ((), ())))
            inv_ref[hi:, :] = inv_ref[hi:, :] - dot(tail, done, (((0,), (0,)), ((), ())))


def inverse_factor(even, odd):
    return pl.pallas_call(
        cholesky_kernel,
        out_shape=jax.ShapeDtypeStruct((PIVOTS, PIVOTS), jnp.float32),
        scratch_shapes=[pltpu.VMEM((PIVOTS, PIVOTS), jnp.float32)],
        compiler_params=pltpu.CompilerParams(vmem_limit_bytes=VMEM_BYTES),
        name="inverse_factor",
    )(even, odd)


def solve_own(own_even, own_odd, inv):
    half = dot(own_even, dot(inv, interleave(0), (((1,), (1,)), ((), ()))), (((1,), (1,)), ((), ())))
    half = half + dot(own_odd, dot(inv, interleave(1), (((1,), (1,)), ((), ()))), (((1,), (1,)), ((), ())))
    return dot(half, inv)


def update_kernel(width, pivot_slots, members, front_ref, even_ref, odd_ref, inv_ref, pivots_ref, rest_ref, factor_ref, lhs):
    @pl.when(pl.program_id(0) == 0)
    def _():
        lhs[...] = solve_own(even_ref[...], odd_ref[...], inv_ref[...])

    p = lax.axis_index("cube") % members
    own = [inv_ref[pl.ds(i * members + p, 1), :] for i in range(pivot_slots)]
    pick = jnp.concatenate(own, 0)
    for k in range(width):
        part = pivots_ref[:, k, :]
        rest_ref[:, k, :] = front_ref[:, k, :] - dot(lhs[...], part)
        factor_ref[:, k, :] = dot(pick, part)


def update(front, even, odd, inv, pivots, pivot_slots, members):
    slots, groups, lanes = front.shape
    width = 8
    whole = lambda j: (0, 0)
    sliced = lambda j: (0, j, 0)
    return pl.pallas_call(
        functools.partial(update_kernel, width, pivot_slots, members),
        grid=(groups // width,),
        out_shape=(
            jax.ShapeDtypeStruct((slots, groups, lanes), jnp.float32),
            jax.ShapeDtypeStruct((pivot_slots, groups, lanes), jnp.float32),
        ),
        in_specs=[
            pl.BlockSpec((slots, width, lanes), sliced),
            pl.BlockSpec((slots, lanes), whole),
            pl.BlockSpec((slots, lanes), whole),
            pl.BlockSpec((PIVOTS, PIVOTS), whole),
            pl.BlockSpec((PIVOTS, width, lanes), sliced),
        ],
        out_specs=(
            pl.BlockSpec((slots, width, lanes), sliced),
            pl.BlockSpec((pivot_slots, width, lanes), sliced),
        ),
        scratch_shapes=[pltpu.VMEM((slots, PIVOTS), jnp.float32)],
        compiler_params=pltpu.CompilerParams(vmem_limit_bytes=VMEM_BYTES),
        name="update_rows",
    )(front, even, odd, inv, pivots)


def both_cores(block):
    parts = lax.all_gather(block, "row", axis=0, tiled=False)
    return parts[0], parts[1]


def eliminate(front, pivot_slots, ny, cut, collective_id):
    members = ny * NX * NZ
    pivots = gather(front[:pivot_slots], ny, cut, collective_id)
    pivots = pivots.reshape(PIVOTS, front.shape[1], LANES)
    even, odd = both_cores(pivots[:, 0, :])
    own_even, own_odd = both_cores(front[:, 0, :])
    inv = inverse_factor(even, odd)
    return update(front, own_even, own_odd, inv, pivots, pivot_slots, members)


def swapped(block):
    count = lax.axis_size("cube")
    return lax.ppermute(block, "cube", [(p, p ^ count // 2) for p in range(count)])


def place_blocks(pieces, mapping):
    targets = lax.broadcasted_iota(jnp.int32, (ROOT_BLOCKS, UPDATE_BLOCKS), 0)
    selector = (targets == mapping[None, :]).astype(jnp.float32)
    spread = jnp.einsum("mu,usvb->msvb", selector, pieces, precision=PRECISE)
    return jnp.einsum("nv,msvb->msnb", selector, spread, precision=PRECISE)


def shards(child_fronts, root_front, child_map):
    position = lax.axis_index("cube")
    half = lax.axis_size("cube") // 2
    child = child_fronts.reshape(child_fronts.shape[1], -1, LANES)
    root = root_front.reshape(root_front.shape[1], -1, LANES)
    child_rest, child_factor = eliminate(child, 4, 2, 2, 1)
    pieces = child_rest[4:, 1:].reshape(UPDATE_BLOCKS, 2, 2, UPDATE_BLOCKS, LANES)
    own_child = position // half
    staying = lax.dynamic_index_in_dim(pieces, own_child, 2, keepdims=False)
    leaving = lax.dynamic_index_in_dim(pieces, 1 - own_child, 2, keepdims=False)
    arrived = swapped(leaving)
    own_map = lax.dynamic_index_in_dim(child_map, own_child, 0, keepdims=False)
    other_map = lax.dynamic_index_in_dim(child_map, 1 - own_child, 0, keepdims=False)
    placed = place_blocks(staying, own_map) + place_blocks(arrived, other_map)
    assembled = root + placed.reshape(root.shape)
    root_rest, root_factor = eliminate(assembled, 2, 4, 1, 2)
    return (
        child_factor.reshape(1, 4, 1, -1),
        root_factor.reshape(1, 2, 1, -1),
        root_rest[2:, 1:].reshape(1, 78, 1, -1),
    )


def solution(mesh):
    placed = P("cube", None, "row", None)
    return jax.shard_map(
        shards, mesh=mesh, in_specs=(placed, placed, P()), out_specs=(placed, placed, placed), check_vma=False
    )
```

time: 678 us -> 185 us (0.27); the launches traced: 667 us -> 183 us
  waiting for transfers between devices: 462 us -> 11 us
  Pallas kernels: 0 us -> 139 us
  other arithmetic: 92.6 us -> 0.36 us
  local copies, waits for them, and re-layouts: 52.5 us -> 17.5 us
  matrix products: 19.3 us -> 3.24 us
  blocking collectives: 24 us -> 7.94 us
  between operations: 14.9 us -> 0.8 us
    all_gather x4 -> x0, waiting for transfers between devices: 449 us -> none  [collect(): gathered = lax.all_gather(pivot_rows, 'cube', axis=0, tiled=True)]
    pallas_call x0 -> x6, Pallas kernels: none -> 139 us  [the longest x2 92.7 us: gather(): pl.pallas_call(functools.partial(gather_kernel, slots, ny, cut), out_shap...]
    another operation x20 -> x0, other arithmetic: 91.4 us -> none  [the longest x12 49.6 us: eliminate(): lower_factor = jnp.linalg.cholesky(diagonal)]
    all_gather x8 -> x4, blocking collectives: 24 us -> 7.94 us  [both_cores(): parts = lax.all_gather(block, 'row', axis=0, tiled=False)]
    all_gather x6 -> x0, local copies, waits for them, and re-layouts: 13.5 us -> none  [the longest x2 13.1 us: collect(): gathered = lax.all_gather(pivot_rows, 'cube', axis=0, tiled=True)]
    another operation x8 -> x0, matrix products: 9.08 us -> none  [the longest x4 8.31 us: eliminate(): lax.linalg.triangular_solve(lower_factor, pivot_block, left_side=True, lo...]
    unnamed x31 -> x4, local copies, waits for them, and re-layouts: 8.58 us -> 0.58 us
    transpose x3 -> x0, local copies, waits for them, and re-layouts: 7.68 us -> none  [eliminate(): pivot_block = jnp.transpose(gathered, (1, 0, 2)).reshape(PANEL, columns)]
  transfers between devices with their start and end apart: 5 -> 1, of which waited for: 5 -> 1; matrix products, arithmetic and copies ran while one was open for 2% -> 1% of each run, Pallas kernels for 0% -> 0%
where the time goes in v1:
time: 185 us; the launch traced here: 183 us
  Pallas kernels  139 us (75%)
  local copies, waits for them, and re-layouts  17.5 us (9%)
  waiting for transfers between devices  11 us (6%)
  blocking collectives  7.94 us (4%)
  starting transfers between devices  3.44 us (2%)
  matrix products  3.24 us (2%)
    pallas_call x2, Pallas kernels, gather(): pl.pallas_call(functools.partial(gather_kernel, slots, ny, cut), out_shap...  92.7 us
    pallas_call x2, Pallas kernels, inverse_factor(): pl.pallas_call(cholesky_kernel, out_shape=jax.ShapeDtypeStruct((PIVOTS, P...  24.5 us
    pallas_call x2, Pallas kernels, update(): pl.pallas_call(functools.partial(update_kernel, width, pivot_slots, membe...  21.3 us
    ppermute x1, waiting for transfers between devices, swapped(): lax.ppermute(block, 'cube', [(p, p ^ count // 2) for p in range(count)])  11 us
    all_gather x4, blocking collectives, both_cores(): parts = lax.all_gather(block, 'row', axis=0, tiled=False)  7.94 us
  transfers between devices with their start and end apart: 1, of which 1 were waited for; matrix products, arithmetic and copies ran while one was open for 1% of the time, Pallas kernels for 0%

profile of v1, /device:TPU:2, one launch (start us, length us, event | category | flops | bytes accessed | tf_op | source)
XLA Modules:
  0.0 182.8 jit_solution(2224328053214508571)
XLA Ops:
  0.6 1.4 slice.54
  2.1 1.0 slice.76
  3.1 1.9 %all-gather = f32[192,1,128]{2,0,1:T(8,128)S(1)} all-gather(f32[96,1,128]{2,0,1:T(8,128)S(1)} %bitcast.66), channel_id=2, replica_groups=mesh['row'=2,'cube'=128] {'row'}, dimensions={0}, use_global_device_ids=true | all-gather | bytes 147456 | tf_op jit(solution)/shard_map/all_gather | solution.py:247
  5.0 0.6 slice_bitcast_fusion.4
  5.6 43.9 %gather_pivot_rows.2 = f32[4,2,4,8,24,128]{5,4,3,2,1,0:T(8,128)} custom-call(f32[4,24,128]{2,1,0:T(8,128)} %bitcast.67), custom_call_target="tpu_custom_call" | custom-call | tf_op jit(solution)/shard_map/gather_pivot_rows/pallas_call | solution.py:112
  49.5 1.3 slice.79
  50.8 2.0 %all-gather.1 = f32[512,1,128]{2,1,0:T(1,128)S(1)} all-gather(f32[256,1,128]{2,1,0:T(1,128)S(1)} %slice.79), channel_id=3, replica_groups=mesh['row'=2,'cube'=128] {'row'}, dimensions={0}, use_global_device_ids=true | all-gather | bytes 393216 | tf_op jit(solution)/shard_map/all_gather | solution.py:247
  52.8 0.7 slice_bitcast_fusion.2
  53.6 12.3 %inverse_factor.2.inv_ref = f32[256,256]{1,0:T(8,128)} custom-call(f32[256,128]{1,0:T(8,128)} %get-tuple-element.25.even_ref, f32[256,128]{1,0:T(8,128)} %get-tuple-element.24.odd_ref), custom_call_target="tpu_custom_call" | custom-call | tf_op jit(solution)/shard_map/inverse_factor/pallas_call | solution.py:188
  65.8 9.2 %update_rows.2 = (f32[96,24,128]{2,1,0:T(8,128)}, f32[4,24,128]{2,1,0:T(8,128)}) custom-call(f32[96,24,128]{2,1,0:T(8,128)} %bitcast.62, f32[96,128]{1,0:T(8,128)} %get-tuple-element.27.even_ref, f32[96,128]{1,0:T(8,128)} %get-tuple-element.26.odd_ref, f32[256,256]{1,0:T(8,128)} %inverse_factor.2.inv_ref, f32[256,24,128]{2,1,0:T(8,128)} %bitcast.57), custom_call_target="tpu_custom_call" | custom-call | tf_op jit(solution)/shard_map/update_rows/pallas_call | solution.py:222
  75.0 1.4 slice.59
  76.7 3.4 %collective-permute-start = (f32[23,2,23,128]{3,1,2,0:T(2,128)S(1)}, f32[23,2,23,128]{3,1,2,0:T(2,128)S(1)}, u32[]{:S(2)}, u32[]{:S(2)}) collective-permute-start(f32[23,2,23,128]{3,1,2,0:T(2,128)S(1)} %bitcast.65), channel_id=1, source_target_pairs={{0,64},{1,65},{2,66},{3,67},{4,68},{5,69},{6,70},{7,71},{8,72},{9,... | collective-permute-start | bytes 1625096 | tf_op jit(solution)/shard_map/ppermute | solution.py:263
  80.2 0.7 fusion.3
  80.9 0.9 fusion.1
  81.8 11.0 %collective-permute-done = f32[23,2,23,128]{3,1,2,0:T(2,128)S(1)} collective-permute-done((f32[23,2,23,128]{3,1,2,0:T(2,128)S(1)}, f32[23,2,23,128]{3,1,2,0:T(2,128)S(1)}, u32[]{:S(2)}, u32[]{:S(2)}) %collective-permute-start) | collective-permute-done | bytes 541728 | tf_op jit(solution)/shard_map/ppermute | solution.py:263
  92.8 0.6 fusion.5
  93.5 1.0 add_bitcast_fusion
  94.5 0.8 copy.29
  95.3 0.6 copy-done
  95.9 0.4 copy_add_fusion
  96.3 1.7 copy.34.front_ref
  98.0 0.6 copy.31.x_ref
  98.6 1.9 %all-gather.2 = f32[160,1,128]{2,0,1:T(8,128)S(1)} all-gather(f32[80,1,128]{2,0,1:T(8,128)S(1)} %slice.82), channel_id=4, replica_groups=mesh['row'=2,'cube'=128] {'row'}, dimensions={0}, use_global_device_ids=true | all-gather | bytes 122880 | tf_op jit(solution)/shard_map/all_gather | solution.py:247
  100.5 0.6 slice_bitcast_fusion.6
  101.1 48.8 %gather_pivot_rows.3 = f32[2,4,4,8,40,128]{5,4,3,2,1,0:T(8,128)} custom-call(f32[2,40,128]{2,1,0:T(8,128)} %copy.31.x_ref), custom_call_target="tpu_custom_call" | custom-call | tf_op jit(solution)/shard_map/gather_pivot_rows/pallas_call | solution.py:112
  149.9 1.3 slice.86
  151.2 2.2 %all-gather.3 = f32[512,1,128]{2,1,0:T(1,128)S(1)} all-gather(f32[256,1,128]{2,1,0:T(1,128)S(1)} %slice.86), channel_id=5, replica_groups=mesh['row'=2,'cube'=128] {'row'}, dimensions={0}, use_global_device_ids=true | all-gather | bytes 393216 | tf_op jit(solution)/shard_map/all_gather | solution.py:247
  153.4 0.7 slice_bitcast_fusion
  154.2 12.2 %inverse_factor.3.inv_ref = f32[256,256]{1,0:T(8,128)} custom-call(f32[256,128]{1,0:T(8,128)} %get-tuple-element.23.even_ref, f32[256,128]{1,0:T(8,128)} %get-tuple-element.22.odd_ref), custom_call_target="tpu_custom_call" | custom-call | tf_op jit(solution)/shard_map/inverse_factor/pallas_call | solution.py:188
  166.4 12.2 %update_rows.3 = (f32[80,40,128]{2,1,0:T(8,128)}, f32[2,40,128]{2,1,0:T(8,128)}) custom-call(f32[80,40,128]{2,1,0:T(8,128)} %copy.34.front_ref, f32[80,128]{1,0:T(8,128)} %get-tuple-element.29.even_ref, f32[80,128]{1,0:T(8,128)} %get-tuple-element.28.odd_ref, f32[256,256]{1,0:T(8,128)} %inverse_factor.3.inv_ref, f32[256,40,128]{2,1,0:T(8,128)} %bitcast.55), custom_call_target="tpu_custom_call" | custom-call | tf_op jit(solution)/shard_map/update_rows/pallas_call | solution.py:222
  178.6 1.6 slice.67
  180.2 2.6 %reshape.65 = f32[1,78,1,4992]{3,2,1,0:T(1,128)} reshape(f32[78,39,128]{2,1,0:T(8,128)S(1)} %slice.67) | data formatting | bytes 3115008 | tf_op jit(solution)/shard_map/reshape | solution.py:292
  (8 shorter events, 0.4 us)
Async XLA Ops:
  76.3 3.8 %copy-start.1 = (s32[2,23]{1,0:T(2,128)S(1)}, s32[2,23]{1,0:T(2,128)}, u32[]{:S(2)}) copy-start(s32[2,23]{1,0:T(2,128)} %param.5) | copy-start | bytes 556
  76.7 16.1 %collective-permute-start = (f32[23,2,23,128]{3,1,2,0:T(2,128)S(1)}, f32[23,2,23,128]{3,1,2,0:T(2,128)S(1)}, u32[]{:S(2)}, u32[]{:S(2)}) collective-permute-start(f32[23,2,23,128]{3,1,2,0:T(2,128)S(1)} %bitcast.65), channel_id=1, source_target_pairs={{0,64},{1,65},{2,66},{3,67},{4,68},{5,69},{6,70},{7,71},{8,72},{9,... | collective-permute-start | bytes 1625096 | tf_op jit(solution)/shard_map/ppermute | solution.py:263
  94.5 1.4 copy-start

commit v2 on v1

v2 whole, which is shorter than its diff:
```python
import functools

import jax
import jax.numpy as jnp
from jax import lax
from jax.experimental import pallas as pl
from jax.experimental.pallas import tpu as pltpu
from jax.sharding import PartitionSpec as P

MESH = pl.DeviceIdType.MESH
LANES = 128
NX = 4
NZ = 8
PIVOTS = 256
UPDATE_BLOCKS = 23
ROOT_BLOCKS = 40
SUB = 64
GROUP = 8
PRECISE = lax.Precision.HIGHEST
VMEM_BYTES = 56 * 2**20
Z_ORDER = (0, 1, 7, 2, 6, 3, 5, 4)
RING = (1, 3, 2)
STRIDE = 3


def dot(a, b, dims=(((1,), (0,)), ((), ()))):
    return lax.dot_general(a, b, dims, precision=PRECISE, preferred_element_type=jnp.float32)


def gather_kernel(
    slots, ny, cut, x_ref, out_ref, inv_ref, own_ref, other_ref,
    d_ref, mine, theirs, diag, diag_other,
    local_sem, slab_sem, z_send, z_recv, p_send, p_recv, s_send, s_recv, t_send, t_recv,
):
    me = lax.axis_index("cube")
    core = lax.axis_index("row")
    z = me % NZ
    x = me // NZ % NX
    y = me // (NZ * NX)
    ly = y % ny
    base = y - ly
    ring_y = RING if ny == 4 else (1,)

    def chip(py, px, pz):
        return (core, (base + py) * (NX * NZ) + px * NZ + pz)

    def over_x(d):
        return chip(ly, (x + d) % NX, z)

    def over_y(d):
        return chip((ly + d) % ny, x, z)

    def over_z(d):
        return chip(ly, x, (z + d) % NZ)

    sibling = (1 - core, me)
    started = []

    def send(src, dst, ssem, rsem, peer):
        copy = pltpu.make_async_remote_copy(
            src_ref=src, dst_ref=dst, send_sem=ssem, recv_sem=rsem, device_id=peer, device_id_type=MESH
        )
        copy.start()
        started.append(copy)
        return copy

    head = x_ref.at[:, pl.ds(0, GROUP)]
    pivot_rows = x_ref.at[pl.ds(0, slots)]
    slab = pltpu.make_async_copy(head, mine, slab_sem)
    slab.start()
    local = pltpu.make_async_copy(pivot_rows, out_ref.at[:, ly, x, z], local_sem)
    local.start()

    barrier = pltpu.get_barrier_semaphore()
    peers = [over_z(d) for d in range(1, NZ)] + [over_x(d) for d in RING] + [over_y(d) for d in ring_y] + [sibling]
    for peer in peers:
        pl.semaphore_signal(barrier, inc=1, device_id=peer, device_id_type=MESH)
    slab.wait()
    diag[ly, x, z] = mine[0:slots, 0, :]
    pl.semaphore_wait(barrier, len(peers))

    def small(stage, k, part, peer):
        return send(part, part, t_send.at[stage, k], t_recv.at[stage, k], peer)

    small_z = [small(0, d, diag.at[ly, x, z], over_z(d)) for d in Z_ORDER[1:]]
    z_copies = {}
    for d in Z_ORDER[1:]:
        z_copies[d] = send(pivot_rows, out_ref.at[:, ly, x, z], z_send.at[d], z_recv.at[d], over_z(d))
    slabs = send(head, theirs, s_send.at[0], s_recv.at[0], sibling)
    local.wait()

    first = pl.ds(0, cut)
    second = pl.ds(cut, slots - cut)
    hops = {}
    thirds = {}
    last = []

    def z_slice(t):
        return (z + NZ - Z_ORDER[t]) % NZ

    def piece(kind, t, k, part, peer):
        return send(part, part, p_send.at[kind, t, k], p_recv.at[kind, t, k], peer)

    def hop(t):
        if t:
            z_copies[Z_ORDER[t]].wait_recv()
        zs = z_slice(t)
        hops[t] = [piece(0, t, k, out_ref.at[first, ly, x, zs], over_x(d)) for k, d in enumerate(RING)]
        hops[t] += [piece(1, t, k, out_ref.at[second, ly, x, zs], over_y(d)) for k, d in enumerate(ring_y)]

    def third(t):
        for copy in hops[t]:
            copy.wait_recv()
        zs = z_slice(t)
        ways = (1, 3) if ny == 4 else ring_y
        thirds[t] = (
            [piece(2, t, k, out_ref.at[first, ly, :, zs], over_y(d)) for k, d in enumerate(ways)],
            [piece(3, t, k, out_ref.at[second, pl.ds(0, ny), x, zs], over_x(d)) for k, d in enumerate((1, 3))],
        )

    def forward(t):
        zs = z_slice(t)
        over_ys, over_xs = thirds[t]
        if ny == 4:
            for k, d in enumerate((1, 3)):
                over_ys[k].wait_recv()
                part = out_ref.at[first, (ly + 4 - d) % 4, pl.ds(2 * k, 2), zs]
                last.append(piece(4, t, k, part, over_y(d)))
        else:
            last.extend(over_ys)
        for k, d in enumerate((1, 3)):
            over_xs[k].wait_recv()
            part = out_ref.at[second, pl.ds(k * (ny // 2), ny // 2), (x + 4 - d) % 4, zs]
            last.append(piece(5, t, k, part, over_x(d)))

    hop(0)
    for copy in small_z:
        copy.wait_recv()
    small_x = [small(1, d, diag.at[ly, x], over_x(d)) for d in RING]
    hop(1)
    hop(2)
    for copy in small_x:
        copy.wait_recv()
    small_y = [small(2, d, diag.at[ly], over_y(d)) for d in ring_y]
    hop(3)
    third(0)
    hop(4)
    third(1)
    for copy in small_y:
        copy.wait_recv()
    small_core = send(diag, diag_other, s_send.at[1], s_recv.at[1], sibling)
    hop(5)
    third(2)
    hop(6)
    third(3)
    slabs.wait_recv()
    own_ref[...] = mine[:, 0, :]
    other_ref[...] = theirs[:, 0, :]
    hop(7)
    small_core.wait_recv()
    d_ref[...] = dot(in_order(diag, slots), interleave(core)) + dot(in_order(diag_other, slots), interleave(1 - core))
    steps = factor_steps(d_ref, inv_ref)
    moves = [functools.partial(forward, 0), functools.partial(third, 4), functools.partial(forward, 1),
             functools.partial(third, 5), functools.partial(forward, 2), functools.partial(third, 6),
             functools.partial(forward, 3), functools.partial(third, 7), functools.partial(forward, 4),
             functools.partial(forward, 5), functools.partial(forward, 6), functools.partial(forward, 7)]
    count = 0
    for _ in steps:
        count += 1
        if count % STRIDE == 0 and moves:
            moves.pop(0)()
    for move in moves:
        move()
    for copy in last:
        copy.wait_recv()
    for copy in started:
        copy.wait_send()


def in_order(diag, slots):
    return jnp.concatenate([diag[:, :, :, i, :].reshape(-1, LANES) for i in range(slots)], 0)


def gather(front, slots, ny, cut, collective_id):
    rows, groups, lanes = front.shape
    anywhere = pl.BlockSpec(memory_space=pl.ANY)
    vmem = pl.BlockSpec(memory_space=pltpu.VMEM)
    diag = pltpu.VMEM((ny, NX, NZ, slots, lanes), jnp.float32)
    slab = pltpu.VMEM((rows, GROUP, lanes), jnp.float32)
    dma = pltpu.SemaphoreType.DMA
    return pl.pallas_call(
        functools.partial(gather_kernel, slots, ny, cut),
        out_shape=(
            jax.ShapeDtypeStruct((slots, ny, NX, NZ, groups, lanes), jnp.float32),
            jax.ShapeDtypeStruct((PIVOTS, PIVOTS), jnp.float32),
            jax.ShapeDtypeStruct((rows, lanes), jnp.float32),
            jax.ShapeDtypeStruct((rows, lanes), jnp.float32),
        ),
        in_specs=[anywhere],
        out_specs=(anywhere, vmem, vmem, vmem),
        scratch_shapes=[
            pltpu.VMEM((PIVOTS, PIVOTS), jnp.float32), slab, slab, diag, diag,
            dma, dma, dma((NZ,)), dma((NZ,)), dma((6, NZ, 3)), dma((6, NZ, 3)),
            dma((2,)), dma((2,)), dma((3, NZ)), dma((3, NZ)),
        ],
        compiler_params=pltpu.CompilerParams(
            collective_id=collective_id, has_side_effects=True, vmem_limit_bytes=VMEM_BYTES
        ),
        name="gather_pivot_rows",
    )(front)


def interleave(parity):
    k = lax.broadcasted_iota(jnp.int32, (LANES, PIVOTS), 0)
    c = lax.broadcasted_iota(jnp.int32, (LANES, PIVOTS), 1)
    return (c == 2 * k + parity).astype(jnp.float32)


def factor_steps(d_ref, inv_ref):
    r = lax.broadcasted_iota(jnp.int32, (PIVOTS, PIVOTS), 0)
    c = lax.broadcasted_iota(jnp.int32, (PIVOTS, PIVOTS), 1)
    inv_ref[...] = (r == c).astype(jnp.float32)
    rs = lax.broadcasted_iota(jnp.int32, (SUB, SUB), 0)
    cs = lax.broadcasted_iota(jnp.int32, (SUB, SUB), 1)
    eye = (rs == cs).astype(jnp.float32)
    sub = lax.broadcasted_iota(jnp.int32, (GROUP, LANES), 0)
    for o in range(PIVOTS // SUB):
        lo, hi = o * SUB, (o + 1) * SUB
        rest = jnp.concatenate([d_ref[lo:hi, lo:hi], eye], 1)
        done = []
        for g in range(SUB // GROUP):
            height = SUB - g * GROUP
            below = lax.broadcasted_iota(jnp.int32, (height, LANES), 0)
            cols = [
                jnp.broadcast_to(rest[:, g * GROUP + k : g * GROUP + k + 1], (height, LANES)) for k in range(GROUP)
            ]
            scale = jnp.zeros((GROUP, LANES), jnp.float32)
            for j in range(GROUP):
                pivot = cols[j][j : j + 1]
                scale = jnp.where(sub == j, jnp.broadcast_to(pivot, (GROUP, LANES)), scale)
                factor = cols[j] * jnp.broadcast_to(1.0 / pivot, (height, LANES))
                factor = jnp.where(below > j, factor, 0.0)
                for k in range(j + 1, GROUP):
                    cols[k] = cols[k] - factor * jnp.broadcast_to(cols[k][j : j + 1], (height, LANES))
                rest = rest - factor * jnp.broadcast_to(rest[j : j + 1], (height, LANES))
            root = lax.rsqrt(scale)
            root = root * (1.5 - 0.5 * scale * root * root)
            done.append(rest[:GROUP] * root)
            rest = rest[GROUP:]
            yield
        small = jnp.concatenate(done, 0)[:, SUB:]
        top = dot(small, inv_ref[lo:hi, :])
        inv_ref[lo:hi, :] = top
        if hi < PIVOTS:
            lead = dot(small, d_ref[lo:hi, :])
            tail = lead[:, hi:]
            d_ref[hi:, :] = d_ref[hi:, :] - dot(tail, lead, (((0,), (0,)), ((), ())))
            inv_ref[hi:, :] = inv_ref[hi:, :] - dot(tail, top, (((0,), (0,)), ((), ())))
        yield


def solve_own(own, other, inv, core):
    across = (((1,), (1,)), ((), ()))
    half = dot(own, dot(inv, interleave(core), across), across)
    half = half + dot(other, dot(inv, interleave(1 - core), across), across)
    return dot(half, inv)


def split(a):
    high = a.astype(jnp.bfloat16)
    return high, (a - high.astype(jnp.float32)).astype(jnp.bfloat16)


def update_kernel(pivot_slots, members, compact, front_ref, own_ref, other_ref, inv_ref, pivots_ref, rest_ref, factor_ref, high_ref, low_ref):
    slots = front_ref.shape[0]
    step = pl.program_id(0)

    @pl.when(step == 0)
    def _():
        core = lax.axis_index("row")
        p = lax.axis_index("cube") % members
        rows = [solve_own(own_ref[...], other_ref[...], inv_ref[...], core)]
        rows += [inv_ref[pl.ds(i * members + p, 1), :] for i in range(pivot_slots)]
        rows += [jnp.zeros((high_ref.shape[0] - slots - pivot_slots, PIVOTS), jnp.float32)]
        high_ref[...], low_ref[...] = split(jnp.concatenate(rows, 0))

    product = functools.partial(jnp.dot, preferred_element_type=jnp.float32)
    for k in range(0, GROUP, 2):
        high, low = split(jnp.concatenate([pivots_ref[:, k, :], pivots_ref[:, k + 1, :]], 1))
        total = product(high_ref[...], high) + (product(high_ref[...], low) + product(low_ref[...], high))
        for e in range(2):
            part = total[:, e * LANES : (e + 1) * LANES]
            rest = front_ref[:, k + e, :] - part[:slots]
            factor_ref[:, k + e, :] = part[slots : slots + pivot_slots]
            if not compact:
                rest_ref[:, k + e, :] = rest
            elif k + e:
                rest_ref[pl.ds(step * GROUP + k + e - 1, slots - pivot_slots, compact), :] = rest[pivot_slots:]
            else:

                @pl.when(step > 0)
                def _():
                    rest_ref[pl.ds(step * GROUP - 1, slots - pivot_slots, compact), :] = rest[pivot_slots:]


def update(front, own, other, inv, pivots, pivot_slots, members, compact):
    slots, groups, lanes = front.shape
    height = -(-(slots + pivot_slots) // 16) * 16
    whole = lambda j: (0, 0)
    sliced = lambda j: (0, j, 0)
    if compact:
        rest_shape = ((slots - pivot_slots) * compact, lanes)
        rest_spec = pl.BlockSpec(rest_shape, whole)
    else:
        rest_shape = (slots, groups, lanes)
        rest_spec = pl.BlockSpec((slots, GROUP, lanes), sliced)
    return pl.pallas_call(
        functools.partial(update_kernel, pivot_slots, members, compact),
        grid=(groups // GROUP,),
        out_shape=(
            jax.ShapeDtypeStruct(rest_shape, jnp.float32),
            jax.ShapeDtypeStruct((pivot_slots, groups, lanes), jnp.float32),
        ),
        in_specs=[
            pl.BlockSpec((slots, GROUP, lanes), sliced),
            pl.BlockSpec((slots, lanes), whole),
            pl.BlockSpec((slots, lanes), whole),
            pl.BlockSpec((PIVOTS, PIVOTS), whole),
            pl.BlockSpec((PIVOTS, GROUP, lanes), sliced),
        ],
        out_specs=(rest_spec, pl.BlockSpec((pivot_slots, GROUP, lanes), sliced)),
        scratch_shapes=[pltpu.VMEM((height, PIVOTS), jnp.bfloat16), pltpu.VMEM((height, PIVOTS), jnp.bfloat16)],
        compiler_params=pltpu.CompilerParams(vmem_limit_bytes=VMEM_BYTES),
        name="update_rows",
    )(front, own, other, inv, pivots)


def eliminate(front, pivot_slots, ny, cut, collective_id, compact):
    members = ny * NX * NZ
    pivots, inv, own, other = gather(front, pivot_slots, ny, cut, collective_id)
    pivots = pivots.reshape(PIVOTS, front.shape[1], LANES)
    return update(front, own, other, inv, pivots, pivot_slots, members, compact)


def swapped(block):
    count = lax.axis_size("cube")
    return lax.ppermute(block, "cube", [(p, p ^ count // 2) for p in range(count)])


def place_blocks(pieces, mapping):
    targets = lax.broadcasted_iota(jnp.int32, (ROOT_BLOCKS, UPDATE_BLOCKS), 0)
    selector = (targets == mapping[None, :]).astype(jnp.float32)
    spread = jnp.einsum("mu,usvb->msvb", selector, pieces, precision=PRECISE)
    return jnp.einsum("nv,msvb->msnb", selector, spread, precision=PRECISE)


def shards(child_fronts, root_front, child_map):
    position = lax.axis_index("cube")
    half = lax.axis_size("cube") // 2
    child = child_fronts.reshape(child_fronts.shape[1], -1, LANES)
    root = root_front.reshape(root_front.shape[1], -1, LANES)
    child_rest, child_factor = eliminate(child, 4, 2, 2, 1, 0)
    pieces = child_rest[4:, 1:].reshape(UPDATE_BLOCKS, 2, 2, UPDATE_BLOCKS, LANES)
    own_child = position // half
    staying = lax.dynamic_index_in_dim(pieces, own_child, 2, keepdims=False)
    leaving = lax.dynamic_index_in_dim(pieces, 1 - own_child, 2, keepdims=False)
    arrived = swapped(leaving)
    own_map = lax.dynamic_index_in_dim(child_map, own_child, 0, keepdims=False)
    other_map = lax.dynamic_index_in_dim(child_map, 1 - own_child, 0, keepdims=False)
    placed = place_blocks(staying, own_map) + place_blocks(arrived, other_map)
    assembled = root + placed.reshape(root.shape)
    root_rest, root_factor = eliminate(assembled, 2, 4, 1, 2, ROOT_BLOCKS - 1)
    return (
        child_factor.reshape(1, 4, 1, -1),
        root_factor.reshape(1, 2, 1, -1),
        root_rest.reshape(1, 78, 1, -1),
    )


def solution(mesh):
    placed = P("cube", None, "row", None)
    return jax.shard_map(
        shards, mesh=mesh, in_specs=(placed, placed, P()), out_specs=(placed, placed, placed), check_vma=False
    )
```

time: 185 us -> 129 us (0.70)
  Pallas kernels: 139 us -> 106 us
  local copies, waits for them, and re-layouts: 17.5 us -> 5.76 us
  blocking collectives: 7.94 us -> 0 us
  waiting for transfers between devices: 11 us -> 7.51 us
    pallas_call x4 -> x2, Pallas kernels: 45.8 us -> 17.7 us  [update(): pl.pallas_call(functools.partial(update_kernel, pivot_slots, members, com...]
    all_gather x4 -> x0, blocking collectives: 7.94 us -> none  [both_cores(): parts = lax.all_gather(block, 'row', axis=0, tiled=False)]
    slice x8 -> x0, local copies, waits for them, and re-layouts: 7.24 us -> none  [the longest x2 2.59 us: eliminate(): even, odd = both_cores(pivots[:, 0, :])]
    pallas_call x2, Pallas kernels: 92.7 us -> 88.7 us  [gather(): pl.pallas_call(functools.partial(gather_kernel, slots, ny, cut), out_shap...]
    ppermute x1, waiting for transfers between devices: 11 us -> 7.51 us  [swapped(): lax.ppermute(block, 'cube', [(p, p ^ count // 2) for p in range(count)])]
    squeeze x4 -> x0, local copies, waits for them, and re-layouts: 2.72 us -> none  [both_cores(): return (parts[0], parts[1])]
    add x2 -> x0, local copies, waits for them, and re-layouts: 2.56 us -> none  [the longest x1 1.71 us: shards(): assembled = root + placed.reshape(root.shape)]
where the time goes in v2:
time: 129 us; the launch traced here: 128 us
  Pallas kernels  106 us (82%)
  waiting for transfers between devices  7.51 us (6%)
  local copies, waits for them, and re-layouts  5.76 us (4%)
  starting transfers between devices  3.25 us (3%)
  matrix products  3.24 us (3%)
  other arithmetic  1.39 us (1%)
    pallas_call x2, Pallas kernels, gather(): pl.pallas_call(functools.partial(gather_kernel, slots, ny, cut), out_shap...  88.7 us
    pallas_call x2, Pallas kernels, update(): pl.pallas_call(functools.partial(update_kernel, pivot_slots, members, com...  17.7 us
    ppermute x1, waiting for transfers between devices, swapped(): lax.ppermute(block, 'cube', [(p, p ^ count // 2) for p in range(count)])  7.51 us
    reshape x1, local copies, waits for them, and re-layouts, shards(): root_rest.reshape(1, 78, 1, -1)  3.57 us
    ppermute x1, starting transfers between devices, swapped(): lax.ppermute(block, 'cube', [(p, p ^ count // 2) for p in range(count)])  3.25 us
  transfers between devices with their start and end apart: 1, of which 1 were waited for; matrix products, arithmetic and copies ran while one was open for 1% of the time, Pallas kernels for 0%

profile of v2, /device:TPU:2, one launch (start us, length us, event | category | flops | bytes accessed | tf_op | source)
XLA Modules:
  0.0 128.3 jit_solution(6430840450947145601)
XLA Ops:
  0.6 42.6 %gather_pivot_rows.2 = (f32[4,2,4,8,24,128]{5,4,3,2,1,0:T(8,128)}, f32[256,256]{1,0:T(8,128)}, f32[96,128]{1,0:T(8,128)}, f32[96,128]{1,0:T(8,128)}) custom-call(f32[96,24,128]{2,1,0:T(8,128)} %bitcast.34), custom_call_target="tpu_custom_call" | custom-call | tf_op jit(solution)/shard_map/gather_pivot_rows/pallas_call | solution.py:191
  43.3 7.5 %update_rows.2 = (f32[96,24,128]{2,1,0:T(8,128)}, f32[4,24,128]{2,1,0:T(8,128)}) custom-call(f32[96,24,128]{2,1,0:T(8,128)} %bitcast.35, f32[96,128]{1,0:T(8,128)} %get-tuple-element.15.own_ref, f32[96,128]{1,0:T(8,128)} %get-tuple-element.16.other_ref, f32[256,256]{1,0:T(8,128)} %get-tuple-element.17.inv_ref, f32[256,24,128]{2,1,0:T(8,128)} %bitcast.37), custom_call_target="tpu_custom_call" | custom-call | tf_op jit(solution)/shard_map/update_rows/pallas_call | solution.py:317
  50.8 1.4 %slice.3 = f32[92,23,128]{2,1,0:T(8,128)S(1)} slice(f32[96,24,128]{2,1,0:T(8,128)} %get-tuple-element.20), slice={[4:96], [1:24], [0:128]} | slice | bytes 2166784 | tf_op jit(solution)/shard_map/slice | solution.py:363
  52.2 0.0 copy-start.1
  52.2 0.1 constant_dynamic-slice_fusion
  52.3 0.3 copy.33
  52.6 3.3 %collective-permute-start = (f32[23,2,23,128]{3,1,2,0:T(2,128)S(1)}, f32[23,2,23,128]{3,1,2,0:T(2,128)S(1)}, u32[]{:S(2)}, u32[]{:S(2)}) collective-permute-start(f32[23,2,23,128]{3,1,2,0:T(2,128)S(1)} %bitcast.39), channel_id=1, source_target_pairs={{0,64},{1,65},{2,66},{3,67},{4,68},{5,69},{6,70},{7,71},{8,72},{9,... | collective-permute-start | bytes 1625096 | tf_op jit(solution)/shard_map/ppermute | solution.py:347
  55.8 0.0 copy-done.1
  55.8 0.7 fusion.3
  56.5 0.9 fusion.1
  57.5 7.5 %collective-permute-done = f32[23,2,23,128]{3,1,2,0:T(2,128)S(1)} collective-permute-done((f32[23,2,23,128]{3,1,2,0:T(2,128)S(1)}, f32[23,2,23,128]{3,1,2,0:T(2,128)S(1)}, u32[]{:S(2)}, u32[]{:S(2)}) %collective-permute-start) | collective-permute-done | bytes 541728 | tf_op jit(solution)/shard_map/ppermute | solution.py:347
  65.0 0.6 fusion.5
  65.6 0.0 copy-start
  65.6 1.0 convolution_add_fusion
  66.6 0.5 copy-done
  67.1 1.4 %bitcast_add_fusion.x_ref.front_ref = f32[80,40,128]{2,1,0:T(8,128)} fusion(f32[80,40,128]{2,1,0:T(8,128)S(1)} %bitcast.38, f32[40,2,128,40]{2,3,1,0:T(8,128)S(1)} %convolution_add_fusion), kind=kLoop, calls=%fused_computation | loop fusion | flops 409600 | bytes 4915200 | tf_op jit(solution)/shard_map/add | solution.py:371
  68.5 46.0 %gather_pivot_rows.3 = (f32[2,4,4,8,40,128]{5,4,3,2,1,0:T(8,128)}, f32[256,256]{1,0:T(8,128)}, f32[80,128]{1,0:T(8,128)}, f32[80,128]{1,0:T(8,128)}) custom-call(f32[80,40,128]{2,1,0:T(8,128)} %bitcast_add_fusion.x_ref.front_ref), custom_call_target="tpu_custom_call" | custom-call | tf_op jit(solution)/shard_map/gather_pivot_rows/pallas_call | solution.py:191
  114.5 10.2 %update_rows.3 = (f32[3042,128]{1,0:T(8,128)}, f32[2,40,128]{2,1,0:T(8,128)}) custom-call(f32[80,40,128]{2,1,0:T(8,128)} %bitcast_add_fusion.x_ref.front_ref, f32[80,128]{1,0:T(8,128)} %get-tuple-element.21.own_ref, f32[80,128]{1,0:T(8,128)} %get-tuple-element.22.other_ref, f32[256,256]{1,0:T(8,128)} %get-tuple-element.23.inv_ref, f32[256,40,128]{2,1,0:T(8,128)} %bitcast.33), custom_call_target="tpu_custom_call" | custom-call | tf_op jit(solution)/shard_map/update_rows/pallas_call | solution.py:317
  124.7 3.6 %reshape.44 = f32[1,78,1,4992]{3,2,1,0:T(1,128)} reshape(f32[3042,128]{1,0:T(8,128)} %get-tuple-element.26) | data formatting | bytes 3115008 | tf_op jit(solution)/shard_map/reshape | solution.py:376
  (1 shorter events, 0.0 us)
Async XLA Ops:
  52.2 3.6 %copy-start.1 = (s32[2,23]{1,0:T(2,128)S(1)}, s32[2,23]{1,0:T(2,128)}, u32[]{:S(2)}) copy-start(s32[2,23]{1,0:T(2,128)} %param.5) | copy-start | bytes 556
  52.6 12.4 %collective-permute-start = (f32[23,2,23,128]{3,1,2,0:T(2,128)S(1)}, f32[23,2,23,128]{3,1,2,0:T(2,128)S(1)}, u32[]{:S(2)}, u32[]{:S(2)}) collective-permute-start(f32[23,2,23,128]{3,1,2,0:T(2,128)S(1)} %bitcast.39), channel_id=1, source_target_pairs={{0,64},{1,65},{2,66},{3,67},{4,68},{5,69},{6,70},{7,71},{8,72},{9,... | collective-permute-start | bytes 1625096 | tf_op jit(solution)/shard_map/ppermute | solution.py:347
  65.6 1.4 %copy-start = (f32[1,80,1,5120]{3,2,1,0:T(1,128)S(1)}, f32[1,80,1,5120]{3,2,1,0:T(1,128)}, u32[]{:S(2)}) copy-start(f32[1,80,1,5120]{3,2,1,0:T(1,128)} %param.4) | copy-start | bytes 4915204

commit v3 on v0

v3 whole, which is shorter than its diff:
```python
import functools

import jax
import jax.numpy as jnp
from jax import lax
from jax.experimental import pallas as pl
from jax.experimental.pallas import tpu as pltpu
from jax.sharding import PartitionSpec as P

MESH = pl.DeviceIdType.MESH
LANES = 128
NX = 4
NZ = 8
PIVOTS = 256
UPDATE_BLOCKS = 23
ROOT_BLOCKS = 40
PIECE_ROWS = 48
SUB = 64
GROUP = 8
PRECISE = lax.Precision.HIGHEST
VMEM_BYTES = 56 * 2**20
Z_ORDER = (0, 1, 7, 2, 6, 3, 5, 4)
RING = (1, 3, 2)


def dot(a, b, dims=(((1,), (0,)), ((), ()))):
    return lax.dot_general(a, b, dims, precision=PRECISE, preferred_element_type=jnp.float32)


def interleave(parity):
    k = lax.broadcasted_iota(jnp.int32, (LANES, PIVOTS), 0)
    c = lax.broadcasted_iota(jnp.int32, (LANES, PIVOTS), 1)
    return (c == 2 * k + parity).astype(jnp.float32)


def factor_steps(d_ref, inv_ref):
    r = lax.broadcasted_iota(jnp.int32, (PIVOTS, PIVOTS), 0)
    c = lax.broadcasted_iota(jnp.int32, (PIVOTS, PIVOTS), 1)
    inv_ref[...] = (r == c).astype(jnp.float32)
    rs = lax.broadcasted_iota(jnp.int32, (SUB, SUB), 0)
    cs = lax.broadcasted_iota(jnp.int32, (SUB, SUB), 1)
    eye = (rs == cs).astype(jnp.float32)
    sub = lax.broadcasted_iota(jnp.int32, (GROUP, LANES), 0)
    for o in range(PIVOTS // SUB):
        lo, hi = o * SUB, (o + 1) * SUB
        rest = jnp.concatenate([d_ref[lo:hi, lo:hi], eye], 1)
        done = []
        for g in range(SUB // GROUP):
            height = SUB - g * GROUP
            below = lax.broadcasted_iota(jnp.int32, (height, LANES), 0)
            cols = [
                jnp.broadcast_to(rest[:, g * GROUP + k : g * GROUP + k + 1], (height, LANES)) for k in range(GROUP)
            ]
            scale = jnp.zeros((GROUP, LANES), jnp.float32)
            for j in range(GROUP):
                pivot = cols[j][j : j + 1]
                scale = jnp.where(sub == j, jnp.broadcast_to(pivot, (GROUP, LANES)), scale)
                factor = cols[j] * jnp.broadcast_to(1.0 / pivot, (height, LANES))
                factor = jnp.where(below > j, factor, 0.0)
                for k in range(j + 1, GROUP):
                    cols[k] = cols[k] - factor * jnp.broadcast_to(cols[k][j : j + 1], (height, LANES))
                rest = rest - factor * jnp.broadcast_to(rest[j : j + 1], (height, LANES))
            root = lax.rsqrt(scale)
            root = root * (1.5 - 0.5 * scale * root * root)
            done.append(rest[:GROUP] * root)
            rest = rest[GROUP:]
            yield
        small = jnp.concatenate(done, 0)[:, SUB:]
        top = dot(small, inv_ref[lo:hi, :])
        inv_ref[lo:hi, :] = top
        if hi < PIVOTS:
            lead = dot(small, d_ref[lo:hi, :])
            tail = lead[:, hi:]
            d_ref[hi:, :] = d_ref[hi:, :] - dot(tail, lead, (((0,), (0,)), ((), ())))
            inv_ref[hi:, :] = inv_ref[hi:, :] - dot(tail, top, (((0,), (0,)), ((), ())))
        yield


class Torus:
    def __init__(self, ny):
        self.me = lax.axis_index("cube")
        self.core = lax.axis_index("row")
        self.ny = ny
        self.z = self.me % NZ
        self.x = self.me // NZ % NX
        self.y = self.me // (NZ * NX)
        self.ly = self.y % ny
        self.base = self.y - self.ly
        self.ring_y = RING if ny == 4 else (1,)
        self.sibling = (1 - self.core, self.me)
        half = lax.axis_size("cube") // 2
        self.across = (self.core, (self.me + half) % (2 * half))
        self.started = []

    def chip(self, py, px, pz):
        return (self.core, (self.base + py) * (NX * NZ) + px * NZ + pz)

    def over_x(self, d):
        return self.chip(self.ly, (self.x + d) % NX, self.z)

    def over_y(self, d):
        return self.chip((self.ly + d) % self.ny, self.x, self.z)

    def over_z(self, d):
        return self.chip(self.ly, self.x, (self.z + d) % NZ)

    def peers(self):
        columns = [self.chip(self.ly, self.x, (self.z + d) % NZ) for d in range(1, NZ)]
        found = columns + [self.sibling]
        found += [self.over_x(d) for d in RING]
        return found + [(self.core, (self.y + d) % 4 * (NX * NZ) + self.x * NZ + self.z) for d in RING]

    def send(self, src, dst, ssem, rsem, peer):
        copy = pltpu.make_async_remote_copy(
            src_ref=src, dst_ref=dst, send_sem=ssem, recv_sem=rsem, device_id=peer, device_id_type=MESH
        )
        copy.start()
        self.started.append(copy)
        return copy


def gather_and_factor(at, first, second, pivots, inv_ref, d_ref, mine, theirs, diag, sems, meanwhile):
    z_send, z_recv, p_send, p_recv, s_send, s_recv, t_send, t_recv = sems
    ny, x, z, ly = at.ny, at.x, at.z, at.ly
    over_x, over_y, over_z = at.over_x, at.over_y, at.over_z

    def small(stage, k, part, peer):
        return at.send(part, part, t_send.at[stage, k], t_recv.at[stage, k], peer)

    own = pivots.at[:, ly, x, z]
    tile = diag.at[at.core, ly, x, z]
    small_z = [small(0, d, tile, over_z(d)) for d in Z_ORDER[1:]]
    z_copies = {d: at.send(own, own, z_send.at[d], z_recv.at[d], over_z(d)) for d in Z_ORDER[1:]}
    blocks = at.send(mine, theirs, s_send, s_recv, at.sibling)
    hops = {}
    thirds = {}
    last = []

    def z_slice(t):
        return (z + NZ - Z_ORDER[t]) % NZ

    def view(part, py, px, t):
        return pivots.at[part[0], py, px, z_slice(t), part[1]]

    def piece(kind, t, k, part, peer):
        return at.send(part, part, p_send.at[kind, t, k], p_recv.at[kind, t, k], peer)

    def hop(t):
        if t:
            z_copies[Z_ORDER[t]].wait_recv()
        hops[t] = [piece(0, t, k, view(first, ly, x, t), over_x(d)) for k, d in enumerate(RING)]
        hops[t] += [piece(1, t, k, view(second, ly, x, t), over_y(d)) for k, d in enumerate(at.ring_y)]

    def third(t):
        for copy in hops[t]:
            copy.wait_recv()
        ways = (1, 3) if ny == 4 else at.ring_y
        thirds[t] = (
            [piece(2, t, k, view(first, ly, pl.ds(0, NX), t), over_y(d)) for k, d in enumerate(ways)],
            [piece(3, t, k, view(second, pl.ds(0, ny), x, t), over_x(d)) for k, d in enumerate((1, 3))],
        )

    def forward(t):
        over_ys, over_xs = thirds[t]
        if ny == 4:
            for k, d in enumerate((1, 3)):
                over_ys[k].wait_recv()
                last.append(piece(4, t, k, view(first, (ly + 4 - d) % 4, pl.ds(2 * k, 2), t), over_y(d)))
        else:
            last.extend(over_ys)
        for k, d in enumerate((1, 3)):
            over_xs[k].wait_recv()
            part = view(second, pl.ds(k * (ny // 2), ny // 2), (x + 4 - d) % 4, t)
            last.append(piece(5, t, k, part, over_x(d)))

    for copy in small_z:
        copy.wait_recv()
    small_x = [small(1, d, diag.at[at.core, ly, x], over_x(d)) for d in RING]
    hop(0)
    hop(1)
    hop(2)
    hop(3)
    hop(4)
    for copy in small_x:
        copy.wait_recv()
    small_y = [small(2, d, diag.at[at.core, ly], over_y(d)) for d in at.ring_y]
    hop(5)
    third(0)
    hop(6)
    third(1)
    third(2)
    hop(7)
    third(3)
    third(4)
    for copy in small_y:
        copy.wait_recv()
    small_core = small(3, 0, diag.at[at.core], at.sibling)
    meanwhile()
    small_core.wait_recv()
    d_ref[...] = dot(in_order(diag, 0), interleave(0)) + dot(in_order(diag, 1), interleave(1))
    moves = {0: ((third, 5), (forward, 0),), 3: ((third, 6), (forward, 1),), 6: ((third, 7), (forward, 2),), 10: ((forward, 3),), 15: ((forward, 4),), 20: ((forward, 5),), 25: ((forward, 6),), 30: ((forward, 7),)}
    for count, _ in enumerate(factor_steps(d_ref, inv_ref)):
        for move, t in moves.pop(count, ()):
            move(t)
    blocks.wait_recv()
    for group in moves.values():
        for move, t in group:
            move(t)

    def finish():
        for copy in last:
            copy.wait_recv()

    return finish


def in_order(diag, core):
    return jnp.concatenate([diag[core, :, :, :, i, :].reshape(-1, LANES) for i in range(diag.shape[4])], 0)


def solve_own(own, other, inv, core):
    across = (((1,), (1,)), ((), ()))
    half = dot(own, dot(inv, interleave(core), across), across)
    half = half + dot(other, dot(inv, interleave(1 - core), across), across)
    return dot(half, inv)


def split(a):
    high = a.astype(jnp.bfloat16)
    return high, (a - high.astype(jnp.float32)).astype(jnp.bfloat16)


def product(left, right):
    mul = functools.partial(jnp.dot, preferred_element_type=jnp.float32)
    (high, low), (top, rest) = left, right
    return mul(high, top) + (mul(high, rest) + mul(low, top))


def left_side(at, slots, pivot_slots, inv_ref, mine, theirs, sides, high_ref, low_ref):
    members = at.ny * NX * NZ
    inv = inv_ref[...]
    top = [-solve_own(mine[...], theirs[...], inv, at.core)] + sides
    rows = [inv_ref[pl.ds(i * members + at.me % members, 1), :] for i in range(pivot_slots)]
    rows += [jnp.zeros((high_ref.shape[0] - slots - pivot_slots, PIVOTS), jnp.float32)]
    below = jnp.concatenate(rows, 0)
    if sides:
        wide = sum(side.shape[1] for side in sides)
        below = jnp.concatenate([below, jnp.zeros((below.shape[0], wide), jnp.float32)], 1)
        top = [jnp.concatenate(top, 1)]
    high_ref[...], low_ref[...] = split(jnp.concatenate(top + [below], 0))


def along_lanes(map_ref, child, shape, per):
    lane = lax.broadcasted_iota(jnp.int32, shape, 1)
    found = jnp.full(shape, -1, jnp.int32)
    for u in range(UPDATE_BLOCKS):
        inside = lane == u + 1 if per == 1 else (lane == 2 * u) | (lane == 2 * u + 1)
        found = jnp.where(inside, map_ref[child, u], found)
    return found


def column_selector(map_ref, child):
    shape = (ROOT_BLOCKS, UPDATE_BLOCKS + 1)
    return (lax.broadcasted_iota(jnp.int32, shape, 0) == along_lanes(map_ref, child, shape, 1)).astype(jnp.float32)


def row_selector(map_ref, child):
    shape = (2 * ROOT_BLOCKS, PIECE_ROWS)
    row = lax.broadcasted_iota(jnp.int32, shape, 0)
    lane = lax.broadcasted_iota(jnp.int32, shape, 1)
    found = along_lanes(map_ref, child, shape, 2)
    return ((found >= 0) & (row == 2 * found + (lane & 1))).astype(jnp.float32)


def kernel(
    place_ref, map_ref, child_ref, root_ref, rest_ref, root_factor_ref, child_factor_ref,
    inv_ref, d_ref, few_own, few_other, held, leave, other, update,
    c_front, c_pivots, c_mine, c_theirs, c_diag, c_high, c_low,
    r_front, r_pivots, r_mine, r_theirs, r_diag, r_high, r_low,
    local_sem, *sems,
):
    c_sems, r_sems, (x_send, x_recv) = sems[:8], sems[8:16], sems[16:]
    at = Torus(2)
    slots, groups = child_ref.shape[0], child_ref.shape[1]
    pivot_slots = child_factor_ref.shape[0]
    whole = pltpu.make_async_copy(child_ref, c_front, local_sem.at[0])
    whole.start()
    local = pltpu.make_async_copy(child_ref.at[pl.ds(0, pivot_slots)], c_pivots.at[:, at.ly, at.x, at.z], local_sem.at[1])
    local.start()
    barrier = pltpu.get_barrier_semaphore()
    peers = at.peers()
    for peer in peers:
        pl.semaphore_signal(barrier, inc=1, device_id=peer, device_id_type=MESH)
    root_whole = pltpu.make_async_copy(root_ref, r_front, local_sem.at[2])
    root_whole.start()
    own_child = at.me // (lax.axis_size("cube") // 2)
    nothing = jnp.zeros((PIECE_ROWS, LANES), jnp.float32)
    held[0] = nothing
    leave[0] = nothing
    row_own, row_other = row_selector(map_ref, own_child), row_selector(map_ref, 1 - own_child)
    col_own, col_other = column_selector(map_ref, own_child), column_selector(map_ref, 1 - own_child)
    whole.wait()
    c_mine[...] = c_front[:, 0, :]
    c_diag[at.core, at.ly, at.x, at.z] = c_front[0:pivot_slots, 0, :]
    local.wait()
    pl.semaphore_wait(barrier, len(peers))

    all_groups = pl.ds(0, groups)
    halves = ((pl.ds(0, 2), all_groups), (pl.ds(2, 2), all_groups))
    finish = gather_and_factor(at, *halves, c_pivots, inv_ref, d_ref, c_mine, c_theirs, c_diag, c_sems, lambda: None)
    left_side(at, slots, pivot_slots, inv_ref, c_mine, c_theirs, [], c_high, c_low)
    left = (c_high[...], c_low[...])
    finish()
    count = (slots - pivot_slots) // 2
    fill = nothing[: PIECE_ROWS - count]
    for k in range(0, groups, 2):
        pair = [c_pivots[:, :, :, :, k + e, :].reshape(PIVOTS, LANES) for e in range(2)]
        total = product(left, split(jnp.concatenate(pair, 1)))
        for e in range(2):
            part = total[:, e * LANES : (e + 1) * LANES]
            child_factor_ref[:, k + e, :] = part[slots : slots + pivot_slots]
            if k + e:
                update[k + e] = c_front[:, k + e, :] + part[:slots]
                even = update[k + e, pl.ds(pivot_slots, count, 2), :]
                odd = update[k + e, pl.ds(pivot_slots + 1, count, 2), :]
                held[k + e] = jnp.concatenate([jnp.where(own_child == 0, even, odd), fill], 0)
                leave[k + e] = jnp.concatenate([jnp.where(own_child == 0, odd, even), fill], 0)

    sent = at.started
    at = Torus(4)
    lead = jnp.maximum(place_ref[own_child, 0], 1)
    blocks = UPDATE_BLOCKS + 1
    for s in range(2):
        few_own[s, 0:blocks] = leave[:, pl.ds(2 * lead - 2 + s, 1), :].reshape(blocks, LANES)
    few_own[2] = leave[lead]
    few = at.send(few_own, few_other, x_send.at[0], x_recv.at[0], at.across)
    root_whole.wait()
    slots, groups = root_ref.shape[0], root_ref.shape[1]
    pivot_slots = root_factor_ref.shape[0]
    lines = []
    for s in range(pivot_slots):
        line = held[:, pl.ds(2 * lead - 2 + s, 1), :].reshape(blocks, LANES)
        lines.append(r_front[s, :, :] + dot(col_own, line))
    column = r_front[:, 0, :] + dot(row_own, held[lead])
    few.wait_recv()
    for s in range(pivot_slots):
        line = lines[s] + dot(col_other, few_other[s, 0:blocks])
        r_pivots[s, at.ly, at.x, at.z] = line
        r_diag[at.core, at.ly, at.x, at.z, s : s + 1, :] = line[0:1]
    r_mine[...] = column + dot(row_other, few_other[2])
    bulk = []

    def exchange():
        bulk.append(at.send(leave, other, x_send.at[1], x_recv.at[1], at.across))

    all_slots = pl.ds(0, pivot_slots)
    halves = ((all_slots, pl.ds(0, 16)), (all_slots, pl.ds(16, groups - 16)))
    finish = gather_and_factor(at, *halves, r_pivots, inv_ref, d_ref, r_mine, r_theirs, r_diag, r_sems, exchange)
    left_side(at, slots, pivot_slots, inv_ref, r_mine, r_theirs, [row_own, row_other], r_high, r_low)
    left = (r_high[...], r_low[...])
    bulk[0].wait_recv()
    finish()
    for k in range(0, groups, 2):
        pair = []
        for n in (k, k + 1):
            pivots = r_pivots[:, :, :, :, n, :].reshape(PIVOTS, LANES)
            kept, arrived = held[place_ref[own_child, n]], other[place_ref[1 - own_child, n]]
            pair.append(jnp.concatenate([pivots, kept, arrived], 0))
        total = product(left, split(jnp.concatenate(pair, 1)))
        for e in range(2):
            part = total[:, e * LANES : (e + 1) * LANES]
            root_factor_ref[:, k + e, :] = part[slots : slots + pivot_slots]
            if k + e:
                rest = r_front[:, k + e, :] + part[:slots]
                rest_ref[pl.ds(k + e - 1, slots - pivot_slots, groups - 1), :] = rest[pivot_slots:]
    for copy in sent + at.started:
        copy.wait_send()


def buffers(front, slots, ny, depth):
    rows, groups, lanes = front.shape
    f32 = jnp.float32
    height = -(-(rows + slots) // 16) * 16
    return [
        pltpu.VMEM((rows, groups, lanes), f32),
        pltpu.VMEM((slots, ny, NX, NZ, groups, lanes), f32),
        pltpu.VMEM((rows, lanes), f32),
        pltpu.VMEM((rows, lanes), f32),
        pltpu.VMEM((2, ny, NX, NZ, slots, lanes), f32),
        pltpu.VMEM((height, depth), jnp.bfloat16),
        pltpu.VMEM((height, depth), jnp.bfloat16),
    ]


def semaphores():
    dma = pltpu.SemaphoreType.DMA
    return [dma((NZ,)), dma((NZ,)), dma((6, NZ, 3)), dma((6, NZ, 3)), dma, dma, dma((4, NZ)), dma((4, NZ))]


def eliminate(place, child_map, child, root):
    f32 = jnp.float32
    lanes = LANES
    dma = pltpu.SemaphoreType.DMA
    anywhere = pl.BlockSpec(memory_space=pl.ANY)
    in_vmem = pl.BlockSpec(memory_space=pltpu.VMEM)
    in_smem = pl.BlockSpec(memory_space=pltpu.SMEM)
    child_slots, root_slots = 4, 2
    few = pltpu.VMEM((3, PIECE_ROWS, lanes), f32)
    piece = pltpu.VMEM((UPDATE_BLOCKS + 1, PIECE_ROWS, lanes), f32)
    return pl.pallas_call(
        kernel,
        out_shape=(
            jax.ShapeDtypeStruct(((root.shape[0] - root_slots) * (root.shape[1] - 1), lanes), f32),
            jax.ShapeDtypeStruct((root_slots, root.shape[1], lanes), f32),
            jax.ShapeDtypeStruct((child_slots, child.shape[1], lanes), f32),
        ),
        in_specs=[in_smem, in_smem, anywhere, anywhere],
        out_specs=(in_vmem, in_vmem, in_vmem),
        scratch_shapes=[
            pltpu.VMEM((PIVOTS, PIVOTS), f32), pltpu.VMEM((PIVOTS, PIVOTS), f32), few, few, piece, piece, piece,
            pltpu.VMEM((child.shape[1], child.shape[0], lanes), f32),
            *buffers(child, child_slots, 2, PIVOTS), *buffers(root, root_slots, 4, PIVOTS + 2 * PIECE_ROWS),
            dma((3,)), *semaphores(), *semaphores(), dma((2,)), dma((2,)),
        ],
        compiler_params=pltpu.CompilerParams(
            collective_id=1, has_side_effects=True, vmem_limit_bytes=VMEM_BYTES
        ),
        name="eliminate_fronts",
    )(place, child_map, child, root)


def shards(child_fronts, root_front, child_map):
    child = child_fronts.reshape(child_fronts.shape[1], -1, LANES)
    root = root_front.reshape(root_front.shape[1], -1, LANES)
    blocks = jnp.arange(ROOT_BLOCKS, dtype=jnp.int32)[None, :, None]
    order = jnp.arange(1, UPDATE_BLOCKS + 1, dtype=jnp.int32)
    place = jnp.max(jnp.where(blocks == child_map[:, None, :], order, 0), 2)
    root_rest, root_factor, child_factor = eliminate(place, child_map, child, root)
    return (
        child_factor.reshape(1, 4, 1, -1),
        root_factor.reshape(1, 2, 1, -1),
        root_rest.reshape(1, 78, 1, -1),
    )


def solution(mesh):
    placed = P("cube", None, "row", None)
    return jax.shard_map(
        shards, mesh=mesh, in_specs=(placed, placed, P()), out_specs=(placed, placed, placed), check_vma=False
    )
```

time: 678 us -> 114 us (0.17); the launches traced: 667 us -> 114 us
  waiting for transfers between devices: 462 us -> 0 us
  Pallas kernels: 0 us -> 107 us
  other arithmetic: 92.6 us -> 0.69 us
  local copies, waits for them, and re-layouts: 52.5 us -> 5.61 us
  blocking collectives: 24 us -> 0 us
  matrix products: 19.3 us -> 0 us
  between operations: 14.9 us -> 0.66 us
    all_gather x4 -> x0, waiting for transfers between devices: 449 us -> none  [collect(): gathered = lax.all_gather(pivot_rows, 'cube', axis=0, tiled=True)]
    pallas_call x0 -> x1, Pallas kernels: none -> 107 us  [eliminate(): pl.pallas_call(kernel, out_shape=(jax.ShapeDtypeStruct(((root.shape[0] -...]
    another operation x20 -> x0, other arithmetic: 91.4 us -> none  [the longest x12 49.6 us: eliminate(): lower_factor = jnp.linalg.cholesky(diagonal)]
    all_gather x8 -> x0, blocking collectives: 24 us -> none  [the longest x4 16.4 us: eliminate(): lax.all_gather(diagonal_half[None], 'row', axis=0, tiled=True)]
    all_gather x6 -> x0, local copies, waits for them, and re-layouts: 13.5 us -> none  [the longest x2 13.1 us: collect(): gathered = lax.all_gather(pivot_rows, 'cube', axis=0, tiled=True)]
    ppermute x1 -> x0, waiting for transfers between devices: 12.2 us -> none  [swapped(): return lax.ppermute(block, axis, route)]
    dot_general x8 -> x0, matrix products: 10.2 us -> none  [the longest x4 7.02 us: eliminate(): jnp.einsum('pr,pc->rc', coupling, factor_block, precision=PRECISE)]
    another operation x8 -> x0, matrix products: 9.08 us -> none  [the longest x4 8.31 us: eliminate(): lax.linalg.triangular_solve(lower_factor, pivot_block, left_side=True, lo...]
  transfers between devices with their start and end apart: 5 -> 0, of which waited for: 5 -> 0; matrix products, arithmetic and copies ran while one was open for 2% -> 0% of each run, Pallas kernels for 0% -> 0%
where the time goes in v3:
time: 114 us
  Pallas kernels  107 us (94%)
  local copies, waits for them, and re-layouts  5.61 us (5%)
    pallas_call x1, Pallas kernels, eliminate(): pl.pallas_call(kernel, out_shape=(jax.ShapeDtypeStruct(((root.shape[0] -...  107 us
    reshape x1, local copies, waits for them, and re-layouts, shards(): root_rest.reshape(1, 78, 1, -1)  3.59 us

profile of v3, /device:TPU:2, one launch (start us, length us, event | category | flops | bytes accessed | tf_op | source)
XLA Modules:
  0.0 113.8 jit_solution(3531082805966509161)
XLA Ops:
  0.6 0.8 copy.12
  1.4 0.7 fusion.place_ref
  2.1 106.8 %eliminate_fronts.1 = (f32[3042,128]{1,0:T(8,128)}, f32[2,40,128]{2,1,0:T(8,128)}, f32[4,24,128]{2,1,0:T(8,128)}) custom-call(s32[2,40]{1,0:T(2,128)} %fusion.place_ref, s32[2,23]{1,0:T(2,128)} %map_ref.1, f32[96,24,128]{2,1,0:T(8,128)} %bitcast.5, f32[80,40,128]{2,1,0:T(8,128)} %bitcast.4), custom_call_target="tpu_custom_call" | custom-call | tf_op jit(solution)/shard_map/eliminate_fronts/pallas_call | solution.py:410
  108.9 0.0 copy-start
  108.9 0.0 copy-start.1
  108.9 3.6 %reshape.27 = f32[1,78,1,4992]{3,2,1,0:T(1,128)} reshape(f32[3042,128]{1,0:T(8,128)} %get-tuple-element.8) | data formatting | bytes 3115008 | tf_op jit(solution)/shard_map/reshape | solution.py:442
  112.5 0.0 copy-done
  112.5 0.6 copy.18
  113.1 0.0 copy-done.1
  113.2 0.6 copy.19
  (1 shorter events, 0.0 us)
Async XLA Ops:
  108.9 3.6 %copy-start = (f32[4,24,128]{2,1,0:T(8,128)S(1)}, f32[4,24,128]{2,1,0:T(8,128)}, u32[]{:S(2)}) copy-start(f32[4,24,128]{2,1,0:T(8,128)} %get-tuple-element.6) | copy-start | bytes 147460
  108.9 4.2 %copy-start.1 = (f32[2,40,128]{2,1,0:T(8,128)S(1)}, f32[2,40,128]{2,1,0:T(8,128)}, u32[]{:S(2)}) copy-start(f32[2,40,128]{2,1,0:T(8,128)} %get-tuple-element.7) | copy-start | bytes 122884

commit v4 on v3

--- a/solution.py
+++ b/solution.py
@@ -119,7 +119,7 @@
         return copy
 
 
-def gather_and_factor(at, first, second, pivots, inv_ref, d_ref, mine, theirs, diag, sems, meanwhile):
+def gather_and_factor(at, first, second, pivots, inv_ref, d_ref, mine, theirs, own_ref, diag, sems, meanwhile):
     z_send, z_recv, p_send, p_recv, s_send, s_recv, t_send, t_recv = sems
     ny, x, z, ly = at.ny, at.x, at.z, at.ly
     over_x, over_y, over_z = at.over_x, at.over_y, at.over_z
@@ -196,13 +196,16 @@
         copy.wait_recv()
     small_core = small(3, 0, diag.at[at.core], at.sibling)
     meanwhile()
+    d_ref[...] = dot(in_order(diag, at.core), interleave(at.core))
+    blocks.wait_recv()
+    own_ref[...] = dot(mine[...], interleave(at.core)) + dot(theirs[...], interleave(1 - at.core))
     small_core.wait_recv()
-    d_ref[...] = dot(in_order(diag, 0), interleave(0)) + dot(in_order(diag, 1), interleave(1))
-    moves = {0: ((third, 5), (forward, 0),), 3: ((third, 6), (forward, 1),), 6: ((third, 7), (forward, 2),), 10: ((forward, 3),), 15: ((forward, 4),), 20: ((forward, 5),), 25: ((forward, 6),), 30: ((forward, 7),)}
+    d_ref[...] = d_ref[...] + dot(in_order(diag, 1 - at.core), interleave(1 - at.core))
+    moves = {0: ((third, 5), (forward, 0)), 2: ((third, 6), (forward, 1)), 4: ((third, 7), (forward, 2))}
+    moves.update({7 + 4 * t: ((forward, 3 + t),) for t in range(5)})
     for count, _ in enumerate(factor_steps(d_ref, inv_ref)):
         for move, t in moves.pop(count, ()):
             move(t)
-    blocks.wait_recv()
     for group in moves.values():
         for move, t in group:
             move(t)
@@ -218,11 +221,8 @@
     return jnp.concatenate([diag[core, :, :, :, i, :].reshape(-1, LANES) for i in range(diag.shape[4])], 0)
 
 
-def solve_own(own, other, inv, core):
-    across = (((1,), (1,)), ((), ()))
-    half = dot(own, dot(inv, interleave(core), across), across)
-    half = half + dot(other, dot(inv, interleave(1 - core), across), across)
-    return dot(half, inv)
+def solve_own(own, inv):
+    return dot(dot(own, inv, (((1,), (1,)), ((), ()))), inv)
 
 
 def split(a):
@@ -236,10 +236,10 @@
     return mul(high, top) + (mul(high, rest) + mul(low, top))
 
 
-def left_side(at, slots, pivot_slots, inv_ref, mine, theirs, sides, high_ref, low_ref):
+def left_side(at, slots, pivot_slots, inv_ref, own_ref, sides, high_ref, low_ref):
     members = at.ny * NX * NZ
     inv = inv_ref[...]
-    top = [-solve_own(mine[...], theirs[...], inv, at.core)] + sides
+    top = [-solve_own(own_ref[...], inv)] + sides
     rows = [inv_ref[pl.ds(i * members + at.me % members, 1), :] for i in range(pivot_slots)]
     rows += [jnp.zeros((high_ref.shape[0] - slots - pivot_slots, PIVOTS), jnp.float32)]
     below = jnp.concatenate(rows, 0)
@@ -275,8 +275,8 @@
 def kernel(
     place_ref, map_ref, child_ref, root_ref, rest_ref, root_factor_ref, child_factor_ref,
     inv_ref, d_ref, few_own, few_other, held, leave, other, update,
-    c_front, c_pivots, c_mine, c_theirs, c_diag, c_high, c_low,
-    r_front, r_pivots, r_mine, r_theirs, r_diag, r_high, r_low,
+    c_front, c_pivots, c_mine, c_theirs, c_own, c_diag, c_high, c_low,
+    r_front, r_pivots, r_mine, r_theirs, r_own, r_diag, r_high, r_low,
     local_sem, *sems,
 ):
     c_sems, r_sems, (x_send, x_recv) = sems[:8], sems[8:16], sems[16:]
@@ -307,8 +307,8 @@
 
     all_groups = pl.ds(0, groups)
     halves = ((pl.ds(0, 2), all_groups), (pl.ds(2, 2), all_groups))
-    finish = gather_and_factor(at, *halves, c_pivots, inv_ref, d_ref, c_mine, c_theirs, c_diag, c_sems, lambda: None)
-    left_side(at, slots, pivot_slots, inv_ref, c_mine, c_theirs, [], c_high, c_low)
+    finish = gather_and_factor(at, *halves, c_pivots, inv_ref, d_ref, c_mine, c_theirs, c_own, c_diag, c_sems, lambda: None)
+    left_side(at, slots, pivot_slots, inv_ref, c_own, [], c_high, c_low)
     left = (c_high[...], c_low[...])
     finish()
     count = (slots - pivot_slots) // 2
@@ -354,9 +354,9 @@
         bulk.append(at.send(leave, other, x_send.at[1], x_recv.at[1], at.across))
 
     all_slots = pl.ds(0, pivot_slots)
-    halves = ((all_slots, pl.ds(0, 16)), (all_slots, pl.ds(16, groups - 16)))
-    finish = gather_and_factor(at, *halves, r_pivots, inv_ref, d_ref, r_mine, r_theirs, r_diag, r_sems, exchange)
-    left_side(at, slots, pivot_slots, inv_ref, r_mine, r_theirs, [row_own, row_other], r_high, r_low)
+    halves = ((all_slots, pl.ds(0, 8)), (all_slots, pl.ds(8, groups - 8)))
+    finish = gather_and_factor(at, *halves, r_pivots, inv_ref, d_ref, r_mine, r_theirs, r_own, r_diag, r_sems, exchange)
+    left_side(at, slots, pivot_slots, inv_ref, r_own, [row_own, row_other], r_high, r_low)
     left = (r_high[...], r_low[...])
     bulk[0].wait_recv()
     finish()
@@ -372,7 +372,7 @@
             root_factor_ref[:, k + e, :] = part[slots : slots + pivot_slots]
             if k + e:
                 rest = r_front[:, k + e, :] + part[:slots]
-                rest_ref[pl.ds(k + e - 1, slots - pivot_slots, groups - 1), :] = rest[pivot_slots:]
+                rest_ref[:, 0, pl.ds((k + e - 1) * LANES, LANES)] = rest[pivot_slots:]
     for copy in sent + at.started:
         copy.wait_send()
 
@@ -386,6 +386,7 @@
         pltpu.VMEM((slots, ny, NX, NZ, groups, lanes), f32),
         pltpu.VMEM((rows, lanes), f32),
         pltpu.VMEM((rows, lanes), f32),
+        pltpu.VMEM((rows, PIVOTS), f32),
         pltpu.VMEM((2, ny, NX, NZ, slots, lanes), f32),
         pltpu.VMEM((height, depth), jnp.bfloat16),
         pltpu.VMEM((height, depth), jnp.bfloat16),
@@ -410,7 +411,7 @@
     return pl.pallas_call(
         kernel,
         out_shape=(
-            jax.ShapeDtypeStruct(((root.shape[0] - root_slots) * (root.shape[1] - 1), lanes), f32),
+            jax.ShapeDtypeStruct((root.shape[0] - root_slots, 1, (root.shape[1] - 1) * lanes), f32),
             jax.ShapeDtypeStruct((root_slots, root.shape[1], lanes), f32),
             jax.ShapeDtypeStruct((child_slots, child.shape[1], lanes), f32),
         ),

time: 114 us -> 113 us (level)
  the two profiles are of different devices: /device:TPU:2 before, /device:TPU:1 now
where the time goes in v4:
time: 113 us
  Pallas kernels  105 us (93%)
  local copies, waits for them, and re-layouts  6.29 us (6%)
    pallas_call x1, Pallas kernels, eliminate(): pl.pallas_call(kernel, out_shape=(jax.ShapeDtypeStruct((root.shape[0] - r...  105 us
    unnamed x4, local copies, waits for them, and re-layouts  6.29 us

profile of v4, /device:TPU:1, one launch (start us, length us, event | category | flops | bytes accessed | tf_op | source)
XLA Modules:
  0.0 112.9 jit_solution(13897738290306110997)
XLA Ops:
  0.6 0.8 copy.8
  1.4 0.7 fusion.place_ref
  2.1 105.3 %eliminate_fronts.1 = (f32[78,1,4992]{2,1,0:T(1,128)}, f32[2,40,128]{2,1,0:T(8,128)}, f32[4,24,128]{2,1,0:T(8,128)}) custom-call(s32[2,40]{1,0:T(2,128)} %fusion.place_ref, s32[2,23]{1,0:T(2,128)} %map_ref.1, f32[96,24,128]{2,1,0:T(8,128)} %bitcast.7, f32[80,40,128]{2,1,0:T(8,128)} %bitcast.5), custom_call_target="tpu_custom_call" | custom-call | tf_op jit(solution)/shard_map/eliminate_fronts/pallas_call | solution.py:411
  107.4 1.4 %copy.14 = f32[1,4,1,3072]{3,2,1,0:T(1,128)} copy(f32[1,4,1,3072]{3,2,1,0:T(1,128)} %bitcast.8) | data formatting | bytes 98304
  108.8 1.4 %copy.15 = f32[1,2,1,5120]{3,2,1,0:T(1,128)} copy(f32[1,2,1,5120]{3,2,1,0:T(1,128)} %bitcast.9) | data formatting | bytes 81920
  110.2 2.7 %copy.16 = f32[1,78,1,4992]{3,2,1,0:T(1,128)} copy(f32[1,78,1,4992]{3,2,1,0:T(1,128)} %bitcast.6) | data formatting | bytes 3115008
  (1 shorter events, 0.0 us)
